TPU v7x, 128 devices: a whole 4x4x4 slice. The times are simulated.
128 devices in a mesh: row: 8 (over y, core), col: 16 (over x, z).
Axes of the slice: x: 4, y: 4, z: 4, core: 2. Of those that a mesh axis runs over, the one named last changes fastest.
Arguments:
- query_embed: bfloat16 [16384, 2048], P('row', 'col'), may hold values from -40 to 40, as said below
- gist_embed: bfloat16 [16384, 2048], P('col', 'row'), may hold values from -40 to 40, as said below
- positive: int32 [16384], P('row'), may hold values from 0 to 16383, each once
Outputs:
- loss_value: float32 [], replicated
- query_grad: float32 [16384, 2048], P('row', 'col')
- gist_grad: float32 [16384, 2048], P('col', 'row')
Inputs may be any that keep to these rules, and one draw needn't show every extreme that they name: `positive`: A permutation of the gist summaries. `query_embed`: Real-valued embeddings. `gist_embed`: Real-valued embeddings.
All inputs are finite; a program needn't handle non-finite values.
Results may differ from a plain program's by a relative error of at most 0.0013.
Values may be sent and summed in bfloat16 or wider, within the bound.
A program may use at most 128 MiB of HBM per device.

v0:
```python
import math

import jax
import jax.numpy as jnp
from jax import lax
from jax.sharding import PartitionSpec as P

D = 2048


def on_device(query_embed, gist_embed, positive):
    query_full = lax.all_gather(query_embed, "col", axis=1, tiled=True)
    gist_full = lax.all_gather(gist_embed, "row", axis=1, tiled=True)
    q_rows = query_full.shape[0]
    g_rows = gist_full.shape[0]
    factor = 1.0 / math.sqrt(D)
    scores = (
        lax.dot_general(
            query_full, gist_full, (((1,), (1,)), ((), ())), preferred_element_type=jnp.float32
        )
        * factor
    )
    col_start = lax.axis_index("col") * g_rows
    onehot_mask = positive[:, None] == col_start + jnp.arange(g_rows, dtype=jnp.int32)[None, :]
    row_max = lax.pmax(jnp.max(scores, axis=1), "col")
    row_total = lax.psum(jnp.sum(jnp.exp(scores - row_max[:, None]), axis=1), "col")
    col_max = lax.pmax(jnp.max(scores, axis=0), "row")
    col_total = lax.psum(jnp.sum(jnp.exp(scores - col_max[None, :]), axis=0), "row")
    row_lse = row_max + jnp.log(row_total)
    col_lse = col_max + jnp.log(col_total)
    onehot = onehot_mask.astype(jnp.float32)
    dlogit = (
        jnp.exp(scores - row_lse[:, None]) + jnp.exp(scores - col_lse[None, :]) - 2.0 * onehot
    ).astype(jnp.bfloat16)
    query_terms = jnp.dot(dlogit, gist_full, preferred_element_type=jnp.float32)
    query_grad = lax.psum_scatter(query_terms, "col", scatter_dimension=1, tiled=True)
    gist_terms = lax.dot_general(
        dlogit, query_full, (((0,), (0,)), ((), ())), preferred_element_type=jnp.float32
    )
    gist_grad = lax.psum_scatter(gist_terms, "row", scatter_dimension=1, tiled=True)
    row_share = q_rows // lax.axis_size("col")
    col_share = g_rows // lax.axis_size("row")
    own_rows = lax.dynamic_slice_in_dim(row_lse, lax.axis_index("col") * row_share, row_share, 0)
    own_cols = lax.dynamic_slice_in_dim(col_lse, lax.axis_index("row") * col_share, col_share, 0)
    local_loss = jnp.sum(own_rows) + jnp.sum(own_cols) - 2.0 * jnp.sum(scores * onehot)
    count_all = q_rows * lax.axis_size("row")
    loss_value = lax.psum(local_loss, ("row", "col")) / (2.0 * count_all)
    return (loss_value, query_grad, gist_grad)


def solution(mesh):
    in_specs = (P("row", "col"), P("col", "row"), P("row"))
    out_specs = (P(), P("row", "col"), P("col", "row"))
    return jax.shard_map(
        on_device, mesh=mesh, in_specs=in_specs, out_specs=out_specs, check_vma=False
    )
```

profile of v0, /device:TPU:1, one launch (start us, length us, event | category | flops | bytes accessed | tf_op | source)
XLA Modules:
  0.0 448.9 jit_solution(14833800560209806136)
XLA Ops:
  7.2 0.0 all-gather.5.cloned.1.call-start
  7.2 0.7 all-gather.5.cloned.1.call-update
  7.9 0.0 all-gather.3.cloned.1.call-start
  7.9 0.7 all-gather.3.cloned.1.call-update
  8.6 0.0 reduce-scatter.5.cloned.1.call-start
  8.7 0.0 copy-start
  8.7 40.7 %all-gather.5.cloned.1.call-done = bf16[1024,2048]{1,0:T(8,128)(2,1)} async-done(((bf16[1024,256]{1,0:T(8,128)(2,1)}), bf16[1024,2048]{1,0:T(8,128)(2,1)}) %all-gather.5.cloned.1.call-update) | async-done | bytes 4194320 | tf_op jit(solution)/shard_map/all_gather | solution.py:13
  49.4 80.3 %all-gather.3.cloned.1.call-done = bf16[2048,2048]{1,0:T(8,128)(2,1)} async-done(((bf16[2048,128]{1,0:T(8,128)(2,1)}), bf16[2048,2048]{1,0:T(8,128)(2,1)}) %all-gather.3.cloned.1.call-update) | async-done | bytes 8388624 | tf_op jit(solution)/shard_map/all_gather | solution.py:12
  129.7 14.6 %multiply_reduce_fusion.1 = (f32[2048]{0:T(1024)S(1)}, f32[2048,1024]{1,0:T(8,128)}) fusion(bf16[2048,2048]{1,0:T(8,128)(2,1)} %all-gather.3.cloned.1.call-done, bf16[1024,2048]{1,0:T(8,128)(2,1)} %all-gather.5.cloned.1.call-done), kind=kOutput, calls=%fused_computation.8 | convolution fusion | flops 8594126848 | bytes 20979712 | tf_op jit(solution)/shard_map/dot_general | solution.py:18
  144.3 31.4 %pmax.14 = f32[2048]{0:T(1024)S(1)} all-reduce(f32[2048]{0:T(1024)S(1)} %get-tuple-element.6), channel_id=1, replica_groups=mesh['row'=8,'col'=16] {'col'}, use_global_device_ids=true, to_apply=%region_1.0 | all-reduce | flops 2048 | bytes 16384 | tf_op jit(solution)/shard_map/pmax | solution.py:25
  175.7 0.0 copy-done
  175.7 8.2 %fusion = (f32[]{:T(128)}, f32[2048]{0:T(1024)S(1)}, f32[1024]{0:T(1024)S(1)}) fusion(f32[2048,1024]{1,0:T(8,128)} %get-tuple-element.7, s32[1024]{0:T(1024)S(1)} %iota_add_fusion, s32[2048]{0:T(1024)S(1)} %copy-done, f32[2048]{0:T(1024)S(1)} %pmax.14), kind=kLoop, calls=%fused_computation.2 | loop fusion | flops 14676991 | bytes 8421380 | tf_op jit(solution)/shard_map/reduce_sum | solution.py:45
  183.9 29.0 %psum.21 = f32[2048]{0:T(1024)S(1)} all-reduce(f32[2048]{0:T(1024)S(1)} %get-tuple-element.4), channel_id=1, replica_groups=mesh['row'=8,'col'=16] {'col'}, use_global_device_ids=true, to_apply=%region_3.0 | all-reduce | flops 2048 | bytes 16384 | tf_op jit(solution)/shard_map/psum | solution.py:26
  213.0 27.5 %pmax.15 = f32[1024]{0:T(1024)S(1)} all-reduce(f32[1024]{0:T(1024)S(1)} %get-tuple-element.5), channel_id=1, replica_groups=mesh['row'=8,'col'=16] {'row'}, use_global_device_ids=true, to_apply=%region_6.0 | all-reduce | flops 1024 | bytes 8192 | tf_op jit(solution)/shard_map/pmax | solution.py:27
  240.5 4.8 %exponential_reduce_fusion = f32[1024]{0:T(1024)S(1)} fusion(f32[2048,1024]{1,0:T(8,128)} %get-tuple-element.7, f32[1024]{0:T(1024)S(1)} %pmax.15), kind=kLoop, calls=%fused_computation.5 | loop fusion | flops 6290432 | bytes 8396800 | tf_op jit(solution)/shard_map/reduce_sum | solution.py:28
  245.3 12.6 %psum.22 = f32[1024]{0:T(1024)S(1)} all-reduce(f32[1024]{0:T(1024)S(1)} %exponential_reduce_fusion), channel_id=1, replica_groups=mesh['row'=8,'col'=16] {'row'}, use_global_device_ids=true, to_apply=%region_8.0 | all-reduce | flops 1024 | bytes 8192 | tf_op jit(solution)/shard_map/psum | solution.py:28
  257.9 20.4 %fusion.3 = f32[1024,2048]{1,0:T(8,128)} fusion(bf16[2048,2048]{1,0:T(8,128)(2,1)} %all-gather.3.cloned.1.call-done, f32[2048,1024]{1,0:T(8,128)} %get-tuple-element.7, f32[1024]{0:T(1024)S(1)} %log_add_fusion.1, f32[2048]{0:T(1024)S(1)} %log_add_fusion, s32[1024]{0:T(1024)S(1)} %iota_add_fusion, s32[2048]{0:T(1024)S(1)} %copy-done), kind=kOutput, calls=%fused_computation.14 | convolution fusion | flops 8606711808 | bytes 25190400 | tf_op jit(solution)/shard_map/dot_general | solution.py:37
  278.3 0.0 reduce-scatter.5.cloned.1.call-update
  278.3 0.3 reduce-scatter.3.cloned.1.call-start
  278.6 17.5 %fusion.5 = f32[2048,2048]{1,0:T(8,128)} fusion(bf16[1024,2048]{1,0:T(8,128)(2,1)} %all-gather.5.cloned.1.call-done, f32[2048,1024]{1,0:T(8,128)} %get-tuple-element.7, f32[1024]{0:T(1024)S(1)} %log_add_fusion.1, f32[2048]{0:T(1024)S(1)} %log_add_fusion, s32[1024]{0:T(1024)S(1)} %iota_add_fusion, s32[2048]{0:T(1024)S(1)} %copy-done), kind=kOutput, calls=%fused_computation.15 | convolution fusion | flops 8606711808 | bytes 29384704 | tf_op jit(solution)/shard_map/dot_general | solution.py:35
  296.1 0.0 reduce-scatter.3.cloned.1.call-update
  296.1 0.7 dynamic-slice_reduce_fusion.1
  296.8 0.7 dynamic-slice_reduce_fusion
  299.3 64.3 %psum.23 = f32[]{:T(128)} all-reduce(f32[]{:T(128)S(6)} %sub.42), channel_id=1, replica_groups=mesh['row'=8,'col'=16] {'row','col'}, use_global_device_ids=true, to_apply=%region_11.0 | all-reduce | flops 1 | bytes 8 | tf_op jit(solution)/shard_map/psum | solution.py:47
  364.3 0.0 reduce-scatter.5.cloned.1.call-done
  364.3 76.9 %reduce-scatter.3.cloned.1.call-done = f32[2048,128]{1,0:T(8,128)} async-done(((f32[2048,2048]{1,0:T(8,128)}), f32[2048,128]{1,0:T(8,128)}) %reduce-scatter.3.cloned.1.call-update) | async-done | bytes 1048592 | tf_op jit(solution)/shard_map/reduce_scatter | solution.py:36
  (3 shorter events, 0.0 us)
Async XLA Ops:
  7.2 42.3 %all-gather.5.cloned.1.call-start = ((), (), s32[]{:S(2)}) async-start(), calls=%async_computation.3 | async-start | bytes 4718592 | tf_op jit(solution)/shard_map/all_gather | solution.py:13
  7.9 121.8 %all-gather.3.cloned.1.call-start = ((), (), s32[]{:S(2)}) async-start(), calls=%async_computation.2 | async-start | bytes 8912896 | tf_op jit(solution)/shard_map/all_gather | solution.py:12
  8.6 355.7 %reduce-scatter.5.cloned.1.call-start = ((), (), s32[]{:S(2)}) async-start(), calls=%async_computation.5 | async-start | bytes 9437184 | tf_op jit(solution)/shard_map/reduce_scatter | solution.py:40
  8.7 167.0 %copy-start = (s32[2048]{0:T(1024)S(1)}, s32[2048]{0:T(1024)}, u32[]{:S(2)}) copy-start(s32[2048]{0:T(1024)} %param.5) | copy-start | bytes 24580
  278.3 162.9 %reduce-scatter.3.cloned.1.call-start = ((), (), s32[]{:S(2)}) async-start(), calls=%async_computation.4 | async-start | bytes 17825792 | tf_op jit(solution)/shard_map/reduce_scatter | solution.py:36
Sparse Core Ops, SparseCore 0:
  9.7 39.6 all-gather.4
  51.5 78.1 all-gather.2
  278.4 47.7 reduce-scatter.4
  330.0 111.1 reduce-scatter.2
where the time goes:
time: 449 us
  waiting for transfers between devices  199 us (44%)
  blocking collectives  165 us (37%)
  matrix products  52.5 us (12%)
  between operations  17.5 us (4%)
  other arithmetic  14.4 us (3%)
    all_gather x1, waiting for transfers between devices, on_device(): query_full = lax.all_gather(query_embed, 'col', axis=1, tiled=True)  80.3 us
    reduce_scatter x1, waiting for transfers between devices, on_device(): lax.psum_scatter(query_terms, 'col', scatter_dimension=1, tiled=True)  76.9 us
    psum x1, blocking collectives, on_device(): loss_value = lax.psum(local_loss, ('row', 'col')) / (2.0 * count_all)  64.3 us
    all_gather x1, waiting for transfers between devices, on_device(): gist_full = lax.all_gather(gist_embed, 'row', axis=1, tiled=True)  40.7 us
    pmax x1, blocking collectives, on_device(): row_max = lax.pmax(jnp.max(scores, axis=1), 'col')  31.4 us
    psum x1, blocking collectives, on_device(): lax.psum(jnp.sum(jnp.exp(scores - row_max[:, None]), axis=1), 'col')  29 us
    pmax x1, blocking collectives, on_device(): col_max = lax.pmax(jnp.max(scores, axis=0), 'row')  27.5 us
    dot_general x1, matrix products, on_device(): lax.dot_general(dlogit, query_full, (((0,), (0,)), ((), ())), preferred_e...  20.4 us
  transfers between devices with their start and end apart: 4, of which 3 were waited for; matrix products, arithmetic and copies ran while one was open for 4% of the time, Pallas kernels for 0%

commit v1 on v0

v1 whole, which is shorter than its diff:
```python
import functools
import math

import jax
import jax.numpy as jnp
from jax import lax
from jax.experimental import pallas as pl
from jax.experimental.pallas import tpu as pltpu
from jax.sharding import PartitionSpec as P

D = 2048
MESH = pl.DeviceIdType.MESH
LOG2E = 1.4426950408889634
LN2 = 0.6931471805599453
F32 = jnp.float32
BF16 = jnp.bfloat16
I16 = jnp.int16
TOP = 32752.0

A, BP, BM, C, DD = 0, 2, 6, 10, 12
R1, R2, R3P, R3M, R4 = 14, 16, 18, 22, 26
NMSG = 28


def where_am_i():
    row = lax.axis_index("row")
    col = lax.axis_index("col")
    return lax.div(col, 4), lax.div(row, 2), lax.rem(col, 4), lax.rem(row, 2)


def mod4(v):
    return lax.rem(v + 8, 4)


def encode(x):
    rows, cols = x.shape
    x3 = x.reshape(rows // 8, 8, cols)
    top = jnp.maximum(jnp.max(jnp.abs(x3), axis=0), 1e-30)
    inv = TOP / top
    code = jnp.round(x3 * inv[None]).reshape(rows, cols).astype(jnp.int32).astype(I16)
    return code, top * (1.0 / TOP)


def decode(code, scale):
    rows, cols = code.shape
    x3 = code.astype(jnp.int32).astype(F32).reshape(rows // 8, 8, cols)
    return (x3 * scale[None]).reshape(rows, cols)


def kernel(
    q_ref, g_ref, pos_ref, loss_ref, qg_ref, gg_ref,
    qbuf, gbuf, s_buf, dl, dlt, posbuf,
    ml, sl, mc, sc, rowst, colst0, colst, rl_t, cl_t, pos_t, pacc,
    qr_s, qr_r, qr_ss, qr_sr, gr_s, gr_r, gr_ss, gr_sr,
    cx_s, cx_r, cx_ss, cx_sr, pg, qout, lossbuf,
    qs, qv, gs, gv, es, ev, ms, mv, rss, rsv, css, csv, ls, lv,
    qss, qsv, gss, gsv, xs, xv, xss, xsv, lsem,
):
    x, y, z, k = where_am_i()
    h = lax.div(x, 2)
    e = lax.rem(x, 2)
    xi = x + 1 - 2 * e
    xo = 3 - x
    xio = 3 - xi
    xj = [x, xo, xi, xio]

    def dev(xx, yy, zz, kk):
        return (yy * 2 + kk, xx * 4 + zz)

    core = dev(x, y, z, 1 - k)
    part_q = dev(xi, y, z, k)
    part_g = dev(xo, y, z, k)
    part_g2 = dev(xo, y, z, 1 - k)
    zpeer = {d: dev(x, y, mod4(z + d), k) for d in (1, 2, 3)}
    ypeer = {d: dev(x, mod4(y + d), z, k) for d in (1, 2, 3)}
    zipeer = {d: dev(xi, y, mod4(z + d), k) for d in (1, 2, 3)}
    yopeer = {d: dev(xo, mod4(y + d), z, k) for d in (1, 2, 3)}
    everyone = [core, part_q, part_g, part_g2]
    for group in (zpeer, ypeer, zipeer, yopeer):
        everyone += list(group.values())

    barrier = pltpu.get_barrier_semaphore()
    for other in everyone:
        pl.semaphore_signal(barrier, inc=1, device_id=other, device_id_type=MESH)

    def rc(src, dst, s, v, to):
        return pltpu.make_async_remote_copy(
            src_ref=src, dst_ref=dst, send_sem=s, recv_sem=v, device_id=to, device_id_type=MESH
        )

    gl = [
        pltpu.make_async_copy(g_ref.at[pl.ds(t * 512, 512)], gbuf.at[y, k, t], lsem.at[t])
        for t in range(2)
    ]
    for c in gl:
        c.start()
    here = pltpu.make_async_copy(q_ref.at[pl.ds(k * 1024, 1024)], qbuf.at[z, 0], lsem.at[2])
    posc = pltpu.make_async_copy(pos_ref, posbuf.at[k], lsem.at[3])
    posc.start()
    pl.semaphore_wait(barrier, len(everyone))

    pos_copy = rc(pos_ref, posbuf.at[k], ms.at[0], mv.at[0], core)
    pos_copy.start()
    q1c = rc(q_ref.at[pl.ds((1 - k) * 1024, 1024)], qbuf.at[z, 0], ms.at[1], mv.at[1], core)
    q1o = [
        rc(q_ref.at[pl.ds(kk * 1024, 1024)], qbuf.at[z, 1], ms.at[2 + kk], mv.at[2],
           dev(xo, y, z, kk))
        for kk in range(2)
    ]

    @pl.when(h == k)
    def _():
        here.start()
        q1c.start()

    @pl.when(h != k)
    def _():
        q1o[0].start()
        q1o[1].start()

    def qp(i, t):
        return qbuf.at[i, t]

    def gp(i, t):
        return gbuf.at[i, k, t]

    def ring(buf, r, sems, semv, plus, minus, partner):
        def msg(src_i, src_t, dst_t, idx, to):
            return rc(buf(src_i, src_t), buf(src_i, dst_t), sems.at[idx], semv.at[idx], to)

        before, after, far = mod4(r - 1), mod4(r + 1), mod4(r + 2)
        m = {}
        for t in range(2):
            m["a", t] = msg(r, t, t + 2, A + t, partner)
            m["d", t] = msg(far, t, t + 2, DD + t, partner)
        for t in range(4):
            m["p", t] = msg(r, t, t, BP + t, plus)
            m["m", t] = msg(r, t, t, BM + t, minus)
        m["c", 0] = msg(before, 0, 0, C, plus)
        m["c", 1] = msg(after, 1, 1, C + 1, minus)
        return m

    qm = ring(qp, z, qs, qv, zpeer[1], zpeer[3], part_q)
    gm = ring(gp, y, gs, gv, ypeer[1], ypeer[3], part_g)

    for c in gl:
        c.wait()
    for t in range(2):
        gm["p", t].start()
        gm["m", t].start()
        gm["a", t].start()

    def to_core(idx, i, t):
        return rc(gp(i, t), gp(i, t), es.at[idx, t], ev.at[idx, t], core)

    ecopies = []

    def start_core(idx, i, t):
        c = to_core(idx, i, t)
        c.start()
        ecopies.append(c)

    start_core(0, y, 0)
    start_core(0, y, 1)

    @pl.when(h == k)
    def _():
        here.wait()

    @pl.when(h != k)
    def _():
        q1c.wait_recv()

    for d in ("p", "m", "a"):
        qm[d, 0].start()
    q1o[0].wait_recv()
    for d in ("p", "m", "a"):
        qm[d, 1].start()

    yb, ya, yf = mod4(y - 1), mod4(y + 1), mod4(y + 2)
    qm["p", 0].wait_recv()
    qm["c", 0].start()
    gm["p", 0].wait_recv()
    gm["c", 0].start()
    start_core(3, yb, 0)
    gm["m", 0].wait_recv()
    start_core(1, ya, 0)
    qm["m", 1].wait_recv()
    qm["c", 1].start()
    gm["m", 1].wait_recv()
    gm["c", 1].start()
    start_core(1, ya, 1)
    gm["p", 1].wait_recv()
    start_core(3, yb, 1)
    for t in range(2):
        qm["a", t].wait_recv()
        qm["p", t + 2].start()
        qm["m", t + 2].start()
        gm["a", t].wait_recv()
        gm["p", t + 2].start()
        gm["m", t + 2].start()
        start_core(0, y, t + 2)
    for t in range(2):
        qm["c", t].wait_recv()
        qm["d", t].start()
        gm["c", t].wait_recv()
        gm["d", t].start()
        start_core(2, yf, t)
    for t in range(2, 4):
        gm["p", t].wait_recv()
        start_core(3, yb, t)
        gm["m", t].wait_recv()
        start_core(1, ya, t)
        qm["p", t].wait_recv()
        qm["m", t].wait_recv()
    qm["m", 0].wait_recv()
    qm["p", 1].wait_recv()
    for t in range(2):
        gm["d", t].wait_recv()
        start_core(2, yf, t + 2)
        qm["d", t].wait_recv()
    for c in ecopies:
        c.wait_recv()
    posc.wait()
    pos_copy.wait_recv()

    scale = LOG2E / math.sqrt(D)

    def logits(t, carry):
        g = jnp.concatenate([gbuf[xj[j], m, t] for j in range(4) for m in range(2)], axis=1)

        def rows_of(b, carry):
            r = pl.ds(pl.multiple_of(b * 256, 256), 256)
            q = jnp.concatenate(
                [qbuf[2 * m + u, j, r, :] for j in range(4) for m in range(2) for u in range(2)],
                axis=1,
            )
            s = lax.dot_general(q, g, (((1,), (1,)), ((), ())), preferred_element_type=F32)
            s = s * scale
            for u in range(4):
                s_buf[t * 4 + u, r, :] = s[:, u * 128:(u + 1) * 128]
            return carry

        return lax.fori_loop(0, 4, rows_of, carry)

    lax.fori_loop(0, 4, logits, 0)

    mc[...] = jnp.full_like(mc, -jnp.inf)
    sc[...] = jnp.zeros_like(sc)

    def stats(a, carry):
        r = pl.ds(pl.multiple_of(a * 128, 128), 128)
        top = s_buf[0, r, :]
        for c in range(1, 16):
            top = jnp.maximum(top, s_buf[c, r, :])
        total = jnp.zeros_like(top)
        for c in range(16):
            v = s_buf[c, r, :]
            total = total + jnp.exp2(v - top)
            v3 = v.reshape(16, 8, 128)
            old = mc[c]
            new = jnp.maximum(old, jnp.max(v3, axis=0))
            mc[c] = new
            sc[c] = sc[c] * jnp.exp2(old - new) + jnp.sum(jnp.exp2(v3 - new[None]), axis=0)
        tt = top.T
        peak = jnp.max(tt, axis=0, keepdims=True)
        one = jnp.sum(total.T * jnp.exp2(tt - peak), axis=0, keepdims=True)
        ml[pl.ds(a, 1), :] = peak
        sl[pl.ds(a, 1), :] = one
        return carry

    lax.fori_loop(0, 8, stats, 0)

    for c in range(16):
        peak = jnp.max(mc[c], axis=0, keepdims=True)
        one = jnp.sum(sc[c] * jnp.exp2(mc[c] - peak), axis=0, keepdims=True)
        colst0[0, c // 8, 0, pl.ds(c % 8, 1), :] = peak
        colst0[0, c // 8, 1, pl.ds(c % 8, 1), :] = one
    ccopy = rc(colst0.at[0], colst0.at[1], ms.at[4], mv.at[4], core)
    ccopy.start()

    me_row = e * 4 + z
    rowst[me_row, 0] = ml[...]
    rowst[me_row, 1] = sl[...]
    rcopies = []
    for d in (1, 2, 3):
        for n, to in ((d - 1, zpeer[d]), (d + 2, zipeer[d])):
            rcopies.append(rc(rowst.at[me_row], rowst.at[me_row], rss.at[n], rsv.at[n], to))
    rcopies.append(rc(rowst.at[me_row], rowst.at[me_row], rss.at[6], rsv.at[6], part_q))
    for c in rcopies:
        c.start()

    ccopy.wait()
    for i in range(2):
        m0, m1 = colst0[0, i, 0], colst0[1, i, 0]
        peak = jnp.maximum(m0, m1)
        colst[0, y, i, 0] = peak
        colst[0, y, i, 1] = colst0[0, i, 1] * jnp.exp2(m0 - peak) + colst0[1, i, 1] * jnp.exp2(
            m1 - peak
        )
    kcopies = []
    for d in (1, 2, 3):
        kcopies.append(rc(colst.at[0, y], colst.at[0, y], css.at[d - 1], csv.at[d - 1], ypeer[d]))
        kcopies.append(rc(colst.at[0, y], colst.at[1, y], css.at[d + 2], csv.at[d + 2], yopeer[d]))
    kcopies.append(rc(colst.at[0, y], colst.at[1, y], css.at[6], csv.at[6], part_g))
    for c in kcopies:
        c.start()

    def pos_cols(a, carry):
        r = pl.ds(pl.multiple_of(a * 128, 128), 128)
        v = posbuf[h, pl.ds(k * 8 + a, 1), :]
        pos_t[r, :] = jnp.broadcast_to(v, (128, 128)).T
        return carry

    lax.fori_loop(0, 8, pos_cols, 0)

    for c in rcopies:
        c.wait()
    peak = rowst[0, 0]
    for n in range(1, 8):
        peak = jnp.maximum(peak, rowst[n, 0])
    tot = jnp.zeros_like(peak)
    for n in range(8):
        tot = tot + rowst[n, 1] * jnp.exp2(rowst[n, 0] - peak)
    row_lse = peak + jnp.log2(tot)
    ml[...] = row_lse

    def row_cols(a, carry):
        r = pl.ds(pl.multiple_of(a * 128, 128), 128)
        rl_t[r, :] = jnp.broadcast_to(ml[pl.ds(a, 1), :], (128, 128)).T
        return carry

    lax.fori_loop(0, 8, row_cols, 0)

    for c in kcopies:
        c.wait()
    for i in range(2):
        peak = colst[0, 0, i, 0]
        for n in range(4):
            peak = jnp.maximum(jnp.maximum(peak, colst[0, n, i, 0]), colst[1, n, 1 - i, 0])
        tot = jnp.zeros_like(peak)
        for n in range(4):
            a0 = colst[0, n, i, 1] * jnp.exp2(colst[0, n, i, 0] - peak)
            a1 = colst[1, n, 1 - i, 1] * jnp.exp2(colst[1, n, 1 - i, 0] - peak)
            tot = tot + (a0 + a1)
        cl_t[pl.ds(i * 8, 8), :] = peak + jnp.log2(tot)

    pacc[...] = jnp.zeros_like(pacc)
    start0 = (x * 4 + z) * 1024
    start1 = (xo * 4 + z) * 1024

    def dlogit(a, carry):
        r = pl.ds(pl.multiple_of(a * 128, 128), 128)
        rl = rl_t[r, :]
        pos = pos_t[r, :]
        lane = lax.broadcasted_iota(jnp.int32, (128, 128), 1)
        acc = jnp.zeros((8, 128), F32)
        for c in range(16):
            base = (start0 if c < 8 else start1) + (c % 8) * 128
            off = pos - base
            v = s_buf[c, r, :]
            hot = off == lane
            p = jnp.exp2(v - rl) + jnp.exp2(v - cl_t[pl.ds(c, 1), :])
            p = jnp.where(hot, p - 2.0, p)
            acc = acc + jnp.sum(jnp.where(hot, v, 0.0).reshape(16, 8, 128), axis=0)
            p = p.astype(BF16)
            dl[r, c * 128:(c + 1) * 128] = p
            dlt[c * 128:(c + 1) * 128, r] = p.T
        pacc[...] += acc
        return carry

    lax.fori_loop(0, 8, dlogit, 0)

    sub = lax.broadcasted_iota(jnp.int32, (8, 128), 0)
    part = jnp.where(sub == me_row, row_lse, 0.0) + jnp.where(sub == y * 2 + k, cl_t[0:8, :], 0.0)
    loss_part = (part - 2.0 * pacc[...]) * LN2
    lcount = [0]

    def loss_pair(v, to):
        n = lcount[0]
        lcount[0] += 1
        lossbuf[2 * n] = v
        c = rc(lossbuf.at[2 * n], lossbuf.at[2 * n + 1], ls.at[n], lv.at[n], to)
        c.start()
        c.wait()
        return v + lossbuf[2 * n + 1]

    def loss_four(v, r, peers, base, sem):
        lossbuf[base + r] = v
        cs = [
            rc(lossbuf.at[base + r], lossbuf.at[base + r], ls.at[sem + d], lv.at[sem + d], peers[d])
            for d in (1, 2, 3)
        ]
        for c in cs:
            c.start()
        for c in cs:
            c.wait()
        return (lossbuf[base] + lossbuf[base + 1]) + (lossbuf[base + 2] + lossbuf[base + 3])

    def grad_q(t):
        for m in range(2):
            g = jnp.concatenate([gbuf[xj[t], m, i] for i in range(4)], axis=0)

            def body(b, carry):
                r = pl.ds(pl.multiple_of(b * 256, 256), 256)
                o = jnp.dot(dl[r, :], g, preferred_element_type=F32)
                s_buf[2 * m * 4 + t, r, :] = o[:, :128]
                s_buf[(2 * m + 1) * 4 + t, r, :] = o[:, 128:]
                return carry

            lax.fori_loop(0, 4, body, 0)

    def grad_g(t, i, kk):
        j = jnp.where(i == x, 0, jnp.where(i == xo, 1, jnp.where(i == xi, 2, 3)))
        q = jnp.concatenate([qbuf[2 * kk, j], qbuf[2 * kk + 1, j]], axis=1)
        return jnp.dot(dlt[t * 512:(t + 1) * 512, :], q, preferred_element_type=F32)

    sent = []

    def send(v, bufs, n, sems, semv, ssems, ssemv, idx, to):
        s, r, ss, sr = bufs
        code, sca = encode(v)
        s[n] = code
        ss[n] = sca
        c1 = rc(s.at[n], r.at[n], sems.at[idx], semv.at[idx], to)
        c2 = rc(ss.at[n], sr.at[n], ssems.at[n], ssemv.at[n], to)
        c1.start()
        c2.start()
        sent.extend((c1, c2))
        return c1, c2

    def take(c, bufs, n):
        c[0].wait_recv()
        c[1].wait_recv()
        return decode(bufs[1][n], bufs[3][n])

    qb = (qr_s, qr_r, qr_ss, qr_sr)
    gb = (gr_s, gr_r, gr_ss, gr_sr)
    B0 = R1

    def sender(bufs, sems, semv, ssems, ssemv):
        return lambda v, idx, to: send(v, bufs, idx - B0, sems, semv, ssems, ssemv, idx, to)

    send_q = sender(qb, qs, qv, qss, qsv)
    send_g = sender(gb, gs, gv, gss, gsv)

    def pq(rel, t):
        return s_buf[mod4(z + rel) * 4 + t]

    def grad_g_foreign(t):
        for rel in range(4):
            code, sca = encode(grad_g(t, mod4(y + rel), 1 - k))
            cx_s[t % 2, rel] = code
            cx_ss[t % 2, rel] = sca
        c1 = rc(cx_s.at[t % 2], cx_r.at[t], xs.at[t], xv.at[t], core)
        c2 = rc(cx_ss.at[t % 2], cx_sr.at[t], xss.at[t], xsv.at[t], core)
        c1.start()
        c2.start()
        return c1, c2

    def reduce_piece(t, get, sendf, plus, minus, partner, msgs, bufs, hold):
        if t >= 2:
            msgs["1", t] = sendf(get(2), R1 + t - 2, partner)
        if t != 0:
            msgs["p", t] = sendf(get(1), R3P + t, plus)
        if t != 1:
            msgs["m", t] = sendf(get(3), R3M + t, minus)
        if t < 2:
            v = get(2) + take(msgs["1", t + 2], bufs, R1 + t - B0)
            msgs["2", t] = sendf(v, R2 + t, plus if t == 0 else minus)

    qmsg, gmsg = {}, {}
    xmsg = {}
    gcache = {}
    for t in (2, 3, 1, 0):
        if t in (1, 0):
            for c in xmsg[t + 2]:
                c.wait_send()
        xmsg[t] = grad_g_foreign(t)
        grad_q(t)
        reduce_piece(t, lambda rel: pq(rel, t), send_q, zpeer[1], zpeer[3], part_q, qmsg, qb, None)
        for c in xmsg[t]:
            c.wait_recv()
        for rel in range(4):
            pg[rel, t] = grad_g(t, mod4(y + rel), k) + decode(cx_r[t, rel], cx_sr[t, rel])
        reduce_piece(t, lambda rel: pg[rel, t], send_g, ypeer[1], ypeer[3], part_g, gmsg, gb, None)
    for t in (1, 0):
        for c in xmsg[t]:
            c.wait_send()

    for msgs, bufs, get, sendf, plus, minus in (
        (qmsg, qb, lambda rel, t: pq(rel, t), send_q, zpeer[1], zpeer[3]),
        (gmsg, gb, lambda rel, t: pg[rel, t], send_g, ypeer[1], ypeer[3]),
    ):
        msgs["m", 1] = sendf(get(3, 1) + take(msgs["2", 1], bufs, R2 + 1 - B0), R3M + 1, minus)
        msgs["p", 0] = sendf(get(1, 0) + take(msgs["2", 0], bufs, R2 - B0), R3P, plus)

    loss = loss_pair(loss_part, core)
    loss = loss_pair(loss, part_q)
    loss = loss_pair(loss, part_g)
    loss = loss_four(loss, z, zpeer, 6, 2)
    loss = loss_four(loss, y, ypeer, 10, 5)
    loss = jnp.sum(jnp.sum(loss, axis=0, keepdims=True), axis=1, keepdims=True)
    loss_ref[...] = jnp.broadcast_to(loss * (1.0 / 32768.0), (8, 128))

    def ring_sum(get, msgs, bufs, t):
        v = get(0, t) + take(msgs["p", t], bufs, R3P + t - B0)
        return v + take(msgs["m", t], bufs, R3M + t - B0)

    for t in (2, 3):
        v = ring_sum(lambda rel, t: pq(rel, t), qmsg, qb, t)
        qmsg["4", t] = send_q(v, R4 + t - 2, part_q)
        v = ring_sum(lambda rel, t: pg[rel, t], gmsg, gb, t)
        gmsg["4", t] = send_g(v, R4 + t - 2, part_g)

    def final(get, msgs, bufs, t):
        v = ring_sum(get, msgs, bufs, t)
        return v + take(msgs["4", t + 2], bufs, R4 + t - B0)

    rows_k = pl.ds(k * 1024, 1024)
    qout[1] = final(lambda rel, t: pq(rel, t), qmsg, qb, 1)
    out_far = rc(qout.at[1], qg_ref.at[rows_k], ms.at[5], mv.at[5 + k], dev(xo, y, z, h))
    out_far.start()
    gg_ref[pl.ds(512, 512), :] = final(lambda rel, t: pg[rel, t], gmsg, gb, 1)
    qout[0] = final(lambda rel, t: pq(rel, t), qmsg, qb, 0)
    out_core = rc(qout.at[0], qg_ref.at[rows_k], ms.at[6], mv.at[5 + k], core)
    out_here = pltpu.make_async_copy(qout.at[0], qg_ref.at[rows_k], lsem.at[4])

    @pl.when(h == k)
    def _():
        out_here.start()

    @pl.when(h != k)
    def _():
        out_core.start()

    gg_ref[pl.ds(0, 512), :] = final(lambda rel, t: pg[rel, t], gmsg, gb, 0)

    def got(kk):
        rc(qout.at[0], qg_ref.at[pl.ds(kk * 1024, 1024)], ms.at[6], mv.at[5 + kk], core).wait_recv()

    @pl.when(h == k)
    def _():
        out_here.wait()
        got(1 - k)
        q1c.wait_send()

    @pl.when(h != k)
    def _():
        out_core.wait_send()
        got(0)
        got(1)
        q1o[0].wait_send()
        q1o[1].wait_send()

    out_far.wait_send()
    pos_copy.wait_send()
    for m in (qm, gm):
        for c in m.values():
            c.wait_send()
    for c in ecopies + sent:
        c.wait_send()


def on_device(query_embed, gist_embed, positive):
    pos = positive.reshape(16, 128)
    vm, dma = pltpu.VMEM, pltpu.SemaphoreType.DMA
    nr = NMSG - R1
    scratch = [
        vm((4, 4, 1024, 128), BF16),
        vm((4, 2, 4, 512, 256), BF16),
        vm((16, 1024, 128), F32),
        vm((1024, 2048), BF16),
        vm((2048, 1024), BF16),
        vm((2, 16, 128), jnp.int32),
        vm((8, 128), F32),
        vm((8, 128), F32),
        vm((16, 8, 128), F32),
        vm((16, 8, 128), F32),
        vm((8, 2, 8, 128), F32),
        vm((2, 2, 2, 8, 128), F32),
        vm((2, 4, 2, 2, 8, 128), F32),
        vm((1024, 128), F32),
        vm((16, 128), F32),
        vm((1024, 128), jnp.int32),
        vm((8, 128), F32),
        vm((nr, 1024, 128), I16),
        vm((nr, 1024, 128), I16),
        vm((nr, 8, 128), F32),
        vm((nr, 8, 128), F32),
        vm((nr, 512, 256), I16),
        vm((nr, 512, 256), I16),
        vm((nr, 8, 256), F32),
        vm((nr, 8, 256), F32),
        vm((2, 4, 512, 256), I16),
        vm((4, 4, 512, 256), I16),
        vm((2, 4, 8, 256), F32),
        vm((4, 4, 8, 256), F32),
        vm((4, 4, 512, 256), F32),
        vm((2, 1024, 128), F32),
        vm((14, 8, 128), F32),
        dma((NMSG,)), dma((NMSG,)),
        dma((NMSG,)), dma((NMSG,)),
        dma((4, 4)), dma((4, 4)),
        dma((8,)), dma((8,)),
        dma((7,)), dma((7,)),
        dma((7,)), dma((7,)),
        dma((9,)), dma((9,)),
        dma((nr,)), dma((nr,)),
        dma((nr,)), dma((nr,)),
        dma((4,)), dma((4,)),
        dma((4,)), dma((4,)),
        dma((5,)),
    ]
    loss, qg, gg = pl.pallas_call(
        kernel,
        out_shape=[
            jax.ShapeDtypeStruct((8, 128), F32),
            jax.ShapeDtypeStruct((2048, 128), F32),
            jax.ShapeDtypeStruct((1024, 256), F32),
        ],
        in_specs=[
            pl.BlockSpec(memory_space=pl.ANY),
            pl.BlockSpec(memory_space=pl.ANY),
            pl.BlockSpec(memory_space=pltpu.VMEM),
        ],
        out_specs=[
            pl.BlockSpec(memory_space=pltpu.VMEM),
            pl.BlockSpec(memory_space=pl.ANY),
            pl.BlockSpec(memory_space=pltpu.VMEM),
        ],
        scratch_shapes=scratch,
        compiler_params=pltpu.CompilerParams(
            collective_id=0, has_side_effects=True, vmem_limit_bytes=63 * 2**20
        ),
    )(query_embed, gist_embed, pos)
    return loss[0, 0], qg, gg


def solution(mesh):
    in_specs = (P("row", "col"), P("col", "row"), P("row"))
    out_specs = (P(), P("row", "col"), P("col", "row"))
    return jax.shard_map(
        on_device, mesh=mesh, in_specs=in_specs, out_specs=out_specs, check_vma=False
    )
```

time: 449 us -> 151 us (0.34)
  waiting for transfers between devices: 199 us -> 0 us
  blocking collectives: 165 us -> 0 us
  Pallas kernels: 0 us -> 146 us
  matrix products: 52.5 us -> 0 us
  between operations: 17.5 us -> 0.64 us
  other arithmetic: 14.4 us -> 0 us
  local copies, waits for them, and re-layouts: 0.01 us -> 4.52 us
    pallas_call x0 -> x1, Pallas kernels: none -> 146 us  [on_device(): pl.pallas_call(kernel, out_shape=[jax.ShapeDtypeStruct((8, 128), F32), ja...]
    all_gather x2 -> x0, waiting for transfers between devices: 121 us -> none  [the longest x1 80.3 us: on_device(): query_full = lax.all_gather(query_embed, 'col', axis=1, tiled=True)]
    psum x3 -> x0, blocking collectives: 106 us -> none  [the longest x1 64.3 us: on_device(): loss_value = lax.psum(local_loss, ('row', 'col')) / (2.0 * count_all)]
    reduce_scatter x2 -> x0, waiting for transfers between devices: 76.9 us -> none  [the longest x1 76.9 us: on_device(): lax.psum_scatter(query_terms, 'col', scatter_dimension=1, tiled=True)]
    pmax x2 -> x0, blocking collectives: 58.9 us -> none  [the longest x1 31.4 us: on_device(): row_max = lax.pmax(jnp.max(scores, axis=1), 'col')]
    dot_general x3 -> x0, matrix products: 52.5 us -> none  [the longest x1 20.4 us: on_device(): lax.dot_general(dlogit, query_full, (((0,), (0,)), ((), ())), preferred_e...]
    reduce_sum x4 -> x0, other arithmetic: 14.4 us -> none  [the longest x1 8.23 us: on_device(): jnp.sum(scores * onehot)]
  transfers between devices with their start and end apart: 4 -> 0, of which waited for: 3 -> 0; matrix products, arithmetic and copies ran while one was open for 4% -> 0% of each run, Pallas kernels for 0% -> 0%
where the time goes in v1:
time: 151 us
  Pallas kernels  146 us (97%)
  local copies, waits for them, and re-layouts  4.52 us (3%)
    pallas_call x1, Pallas kernels, on_device(): pl.pallas_call(kernel, out_shape=[jax.ShapeDtypeStruct((8, 128), F32), ja...  146 us
    unnamed x4, local copies, waits for them, and re-layouts  3.32 us

profile of v1, /device:TPU:1, one launch (start us, length us, event | category | flops | bytes accessed | tf_op | source)
XLA Modules:
  0.0 150.8 jit_solution(16328936117349244835)
XLA Ops:
  0.6 145.6 %shard_map.58 = (f32[8,128]{1,0:T(8,128)}, f32[2048,128]{1,0:T(8,128)}, f32[1024,256]{1,0:T(8,128)}) custom-call(bf16[2048,128]{1,0:T(8,128)(2,1)} %q_ref.1, bf16[1024,256]{1,0:T(8,128)(2,1)} %g_ref.1, s32[16,128]{1,0:T(8,128)} %bitcast.2), custom_call_target="tpu_custom_call" | custom-call | tf_op jit(solution)/shard_map/pallas_call | solution.py:615
  146.2 1.2 slice.3
  147.4 0.0 copy-start
  147.4 2.4 %copy.8 = f32[2048,128]{1,0:T(8,128)} copy(f32[2048,128]{1,0:T(8,128)} %get-tuple-element.13) | data formatting | bytes 2097152
  149.8 0.0 copy-done
  149.8 1.0 copy.9
Async XLA Ops:
  147.4 2.4 %copy-start = (f32[1024,256]{1,0:T(8,128)S(1)}, f32[1024,256]{1,0:T(8,128)}, u32[]{:S(2)}) copy-start(f32[1024,256]{1,0:T(8,128)} %get-tuple-element.14) | copy-start | bytes 3145732

commit v2 on v1

v2 whole, which is shorter than its diff:
```python
import functools
import math

import jax
import jax.numpy as jnp
from jax import lax
from jax.experimental import pallas as pl
from jax.experimental.pallas import tpu as pltpu
from jax.sharding import PartitionSpec as P

D = 2048
MESH = pl.DeviceIdType.MESH
LOG2E = 1.4426950408889634
LN2 = 0.6931471805599453
F32 = jnp.float32
BF16 = jnp.bfloat16
I16 = jnp.int16
TOP = 32752.0

A, BP, BM, C, DD, NGATHER = 0, 4, 12, 20, 24, 28
R1, R3P, R3M, R2, R3PH, R3MH, R4, NSLOT = 0, 4, 8, 12, 16, 20, 24, 28
OUT = R4


def where_am_i():
    row = lax.axis_index("row")
    col = lax.axis_index("col")
    return lax.div(col, 4), lax.div(row, 2), lax.rem(col, 4), lax.rem(row, 2)


def mod4(v):
    return lax.rem(v + 8, 4)


def encode(x):
    rows, cols = x.shape
    x3 = x.reshape(rows // 8, 8, cols)
    top = jnp.maximum(jnp.max(jnp.abs(x3), axis=0), 1e-30)
    inv = TOP / top
    code = jnp.round(x3 * inv[None]).reshape(rows, cols).astype(jnp.int32).astype(I16)
    return code, top * (1.0 / TOP)


def decode(code, scale):
    rows, cols = code.shape
    x3 = code.astype(jnp.int32).astype(F32).reshape(rows // 8, 8, cols)
    return (x3 * scale[None]).reshape(rows, cols)


def kernel(
    q_ref, g_ref, pos_ref, loss_ref, qg_ref, gg_ref,
    qbuf, gbuf, s_buf, dl, dlt, posbuf,
    ml, sl, mc, sc, rowst, colst0, colst, cl_t, pacc,
    qr_s, qr_r, qr_ss, qr_sr, gr_s, gr_r, gr_ss, gr_sr,
    cx_s, cx_r, cx_ss, cx_sr, pg, qout, gout, qo_r, qo_sr, lossbuf,
    qs, qv, gs, gv, es, ev, ms, mv, rss, rsv, css, csv, ls, lv,
    qcs, qcv, qss, qsv, gcs, gcv, gss, gsv, xs, xv, xss, xsv, ov, ovs, lsem, osem,
):
    x, y, z, k = where_am_i()
    h = lax.div(x, 2)
    e = lax.rem(x, 2)
    xi = x + 1 - 2 * e
    xo = 3 - x
    xio = 3 - xi
    xj = [x, xo, xi, xio]

    def dev(xx, yy, zz, kk):
        return (yy * 2 + kk, xx * 4 + zz)

    core = dev(x, y, z, 1 - k)
    part_q = dev(xi, y, z, k)
    part_g = dev(xo, y, z, k)
    part_g2 = dev(xo, y, z, 1 - k)
    zpeer = {d: dev(x, y, mod4(z + d), k) for d in (1, 2, 3)}
    ypeer = {d: dev(x, mod4(y + d), z, k) for d in (1, 2, 3)}
    zipeer = {d: dev(xi, y, mod4(z + d), k) for d in (1, 2, 3)}
    yopeer = {d: dev(xo, mod4(y + d), z, k) for d in (1, 2, 3)}
    everyone = [core, part_q, part_g, part_g2]
    for group in (zpeer, ypeer, zipeer, yopeer):
        everyone += list(group.values())

    barrier = pltpu.get_barrier_semaphore()
    for other in everyone:
        pl.semaphore_signal(barrier, inc=1, device_id=other, device_id_type=MESH)

    def rc(src, dst, s, v, to):
        return pltpu.make_async_remote_copy(
            src_ref=src, dst_ref=dst, send_sem=s, recv_sem=v, device_id=to, device_id_type=MESH
        )

    gl = [
        pltpu.make_async_copy(g_ref.at[pl.ds(t * 512, 512)], gbuf.at[y, k, t], lsem.at[t])
        for t in range(2)
    ]
    for c in gl:
        c.start()
    here = pltpu.make_async_copy(q_ref.at[pl.ds(k * 1024, 1024)], qbuf.at[z, 0], lsem.at[2])
    posc = pltpu.make_async_copy(pos_ref, posbuf.at[k], lsem.at[3])
    posc.start()
    pl.semaphore_wait(barrier, len(everyone))

    pos_copy = rc(pos_ref, posbuf.at[k], ms.at[0], mv.at[0], core)
    pos_copy.start()
    q1c = rc(q_ref.at[pl.ds((1 - k) * 1024, 1024)], qbuf.at[z, 0], ms.at[1], mv.at[1], core)
    q1o = [
        rc(q_ref.at[pl.ds(kk * 1024 + u * 512, 512)], qbuf.at[z, 1, pl.ds(u * 512, 512)],
           ms.at[2 + kk * 2 + u], mv.at[2 + u], dev(xo, y, z, kk))
        for u in range(2) for kk in range(2)
    ]

    @pl.when(h == k)
    def _():
        here.start()
        q1c.start()

    @pl.when(h != k)
    def _():
        for c in q1o:
            c.start()

    def qp(i, t, u):
        return qbuf.at[i, t, pl.ds(u * 512, 512)]

    def gp(i, t, u):
        return gbuf.at[i, k, t, pl.ds(u * 256, 256)]

    def ring(buf, r, sems, semv, plus, minus, partner):
        def msg(i, t, u, t2, idx, to):
            return rc(buf(i, t, u), buf(i, t2, u), sems.at[idx], semv.at[idx], to)

        before, after, far = mod4(r - 1), mod4(r + 1), mod4(r + 2)
        m = {}
        for t in range(4):
            for u in range(2):
                n = t * 2 + u
                if t < 2:
                    m["a", t, u] = msg(r, t, u, t + 2, A + n, partner)
                    m["d", t, u] = msg(far, t, u, t + 2, DD + n, partner)
                    m["c", t, u] = msg(before if u == 0 else after, t, u, t, C + n,
                                       plus if u == 0 else minus)
                m["p", t, u] = msg(r, t, u, t, BP + n, plus)
                m["m", t, u] = msg(r, t, u, t, BM + n, minus)
        return m

    qm = ring(qp, z, qs, qv, zpeer[1], zpeer[3], part_q)
    gm = ring(gp, y, gs, gv, ypeer[1], ypeer[3], part_g)
    yb, ya, yf = mod4(y - 1), mod4(y + 1), mod4(y + 2)
    ecopies = []

    def start_core(idx, i, t, u):
        c = rc(gp(i, t, u), gp(i, t, u), es.at[idx, t, u], ev.at[idx, t, u], core)
        c.start()
        ecopies.append(c)

    def both(m, t, first):
        u = first
        m["p", t, u].start()
        m["m", t, 1 - u].start()

    def on(m, t):
        m["p", t, 0].wait_recv()
        m["c", t, 0].start()
        m["m", t, 1].wait_recv()
        m["c", t, 1].start()

    for c in gl:
        c.wait()
    both(gm, 0, 0)
    both(gm, 0, 1)
    for t in range(2):
        for u in range(2):
            gm["a", t, u].start()
    both(gm, 1, 0)

    @pl.when(h == k)
    def _():
        here.wait()

    @pl.when(h != k)
    def _():
        q1c.wait_recv()

    both(qm, 0, 0)
    both(qm, 0, 1)
    for u in range(2):
        qm["a", 0, u].start()
    for t in range(2):
        for u in range(2):
            start_core(0, y, t, u)
    on(gm, 0)
    on(qm, 0)
    both(gm, 1, 1)
    q1o[0].wait_recv()
    q1o[2].wait_recv()
    both(qm, 1, 0)
    qm["a", 1, 0].start()
    both(qm, 1, 1)
    qm["a", 1, 1].start()
    start_core(3, yb, 0, 0)
    start_core(1, ya, 0, 1)
    gm["p", 0, 1].wait_recv()
    start_core(3, yb, 0, 1)
    gm["m", 0, 0].wait_recv()
    start_core(1, ya, 0, 0)
    on(gm, 1)
    start_core(3, yb, 1, 0)
    start_core(1, ya, 1, 1)
    for u in range(2):
        gm["c", 0, u].wait_recv()
        gm["d", 0, u].start()
        start_core(2, yf, 0, u)
        qm["c", 0, u].wait_recv()
        qm["d", 0, u].start()
    on(qm, 1)
    for u in range(2):
        gm["a", 0, u].wait_recv()
        gm["p", 2, u].start()
        gm["m", 2, u].start()
        start_core(0, y, 2, u)
        qm["a", 0, u].wait_recv()
        qm["p", 2, u].start()
        qm["m", 2, u].start()
    gm["p", 1, 1].wait_recv()
    start_core(3, yb, 1, 1)
    gm["m", 1, 0].wait_recv()
    start_core(1, ya, 1, 0)
    for u in range(2):
        qm["a", 1, u].wait_recv()
        qm["p", 3, u].start()
        qm["m", 3, u].start()
        gm["a", 1, u].wait_recv()
        gm["p", 3, u].start()
        gm["m", 3, u].start()
        start_core(0, y, 3, u)
    for u in range(2):
        gm["c", 1, u].wait_recv()
        gm["d", 1, u].start()
        start_core(2, yf, 1, u)
        qm["c", 1, u].wait_recv()
        qm["d", 1, u].start()
    for t in range(2, 4):
        for u in range(2):
            gm["p", t, u].wait_recv()
            start_core(3, yb, t, u)
            gm["m", t, u].wait_recv()
            start_core(1, ya, t, u)
            gm["d", t - 2, u].wait_recv()
            start_core(2, yf, t, u)
    for t in range(4):
        for u in range(2):
            if t >= 2 or u == 1:
                qm["p", t, u].wait_recv()
            if t >= 2 or u == 0:
                qm["m", t, u].wait_recv()
            if t < 2:
                qm["d", t, u].wait_recv()
    for c in ecopies:
        c.wait_recv()
    posc.wait()
    pos_copy.wait_recv()

    scale = LOG2E / math.sqrt(D)

    def logits(t, carry):
        g = jnp.concatenate([gbuf[xj[j], m, t] for j in range(4) for m in range(2)], axis=1)

        q = jnp.concatenate(
            [qbuf[2 * m + u, j] for j in range(4) for m in range(2) for u in range(2)], axis=1
        )
        s = lax.dot_general(q, g, (((1,), (1,)), ((), ())), preferred_element_type=F32)
        s = s * scale
        for u in range(4):
            s_buf[t * 4 + u] = s[:, u * 128:(u + 1) * 128]
        return carry

    lax.fori_loop(0, 4, logits, 0)

    mc[...] = jnp.full_like(mc, -jnp.inf)
    sc[...] = jnp.zeros_like(sc)

    def stats(a, carry):
        r = pl.ds(pl.multiple_of(a * 128, 128), 128)
        top = s_buf[0, r, :]
        for c in range(1, 16):
            top = jnp.maximum(top, s_buf[c, r, :])
        total = jnp.zeros_like(top)
        for c in range(16):
            v = s_buf[c, r, :]
            total = total + jnp.exp2(v - top)
            v3 = v.reshape(16, 8, 128)
            old = mc[c]
            new = jnp.maximum(old, jnp.max(v3, axis=0))
            mc[c] = new
            sc[c] = sc[c] * jnp.exp2(old - new) + jnp.sum(jnp.exp2(v3 - new[None]), axis=0)
        tt = top.T
        peak = jnp.max(tt, axis=0, keepdims=True)
        one = jnp.sum(total.T * jnp.exp2(tt - peak), axis=0, keepdims=True)
        ml[pl.ds(a, 1), :] = peak
        sl[pl.ds(a, 1), :] = one
        return carry

    lax.fori_loop(0, 8, stats, 0)

    for c in range(16):
        peak = jnp.max(mc[c], axis=0, keepdims=True)
        one = jnp.sum(sc[c] * jnp.exp2(mc[c] - peak), axis=0, keepdims=True)
        colst0[0, c // 8, 0, pl.ds(c % 8, 1), :] = peak
        colst0[0, c // 8, 1, pl.ds(c % 8, 1), :] = one
    ccopy = rc(colst0.at[0], colst0.at[1], ms.at[6], mv.at[4], core)
    ccopy.start()

    me_row = e * 4 + z
    rowst[me_row, 0] = ml[...]
    rowst[me_row, 1] = sl[...]
    rcopies = []
    for d in (1, 2, 3):
        for n, to in ((d - 1, zpeer[d]), (d + 2, zipeer[d])):
            rcopies.append(rc(rowst.at[me_row], rowst.at[me_row], rss.at[n], rsv.at[n], to))
    rcopies.append(rc(rowst.at[me_row], rowst.at[me_row], rss.at[6], rsv.at[6], part_q))
    for c in rcopies:
        c.start()

    ccopy.wait()
    for i in range(2):
        m0, m1 = colst0[0, i, 0], colst0[1, i, 0]
        peak = jnp.maximum(m0, m1)
        colst[0, y, i, 0] = peak
        colst[0, y, i, 1] = colst0[0, i, 1] * jnp.exp2(m0 - peak) + colst0[1, i, 1] * jnp.exp2(
            m1 - peak
        )
    kcopies = []
    for d in (1, 2, 3):
        kcopies.append(rc(colst.at[0, y], colst.at[0, y], css.at[d - 1], csv.at[d - 1], ypeer[d]))
        kcopies.append(rc(colst.at[0, y], colst.at[1, y], css.at[d + 2], csv.at[d + 2], yopeer[d]))
    kcopies.append(rc(colst.at[0, y], colst.at[1, y], css.at[6], csv.at[6], part_g))
    for c in kcopies:
        c.start()

    for c in rcopies:
        c.wait()
    peak = rowst[0, 0]
    for n in range(1, 8):
        peak = jnp.maximum(peak, rowst[n, 0])
    tot = jnp.zeros_like(peak)
    for n in range(8):
        tot = tot + rowst[n, 1] * jnp.exp2(rowst[n, 0] - peak)
    row_lse = peak + jnp.log2(tot)
    ml[...] = row_lse

    for c in kcopies:
        c.wait()
    for i in range(2):
        peak = colst[0, 0, i, 0]
        for n in range(4):
            peak = jnp.maximum(jnp.maximum(peak, colst[0, n, i, 0]), colst[1, n, 1 - i, 0])
        tot = jnp.zeros_like(peak)
        for n in range(4):
            a0 = colst[0, n, i, 1] * jnp.exp2(colst[0, n, i, 0] - peak)
            a1 = colst[1, n, 1 - i, 1] * jnp.exp2(colst[1, n, 1 - i, 0] - peak)
            tot = tot + (a0 + a1)
        cl_t[pl.ds(i * 8, 8), :] = peak + jnp.log2(tot)

    pacc[...] = jnp.zeros_like(pacc)
    start0 = (x * 4 + z) * 1024
    start1 = (xo * 4 + z) * 1024

    def dlogit(a, carry):
        r = pl.ds(pl.multiple_of(a * 128, 128), 128)
        rl = jnp.broadcast_to(ml[pl.ds(a, 1), :], (128, 128)).T
        pos = jnp.broadcast_to(posbuf[h, pl.ds(k * 8 + a, 1), :], (128, 128)).T
        lane = lax.broadcasted_iota(jnp.int32, (128, 128), 1)
        acc = jnp.zeros((8, 128), F32)
        for c in range(16):
            base = (start0 if c < 8 else start1) + (c % 8) * 128
            off = pos - base
            v = s_buf[c, r, :]
            hot = off == lane
            p = jnp.exp2(v - rl) + jnp.exp2(v - cl_t[pl.ds(c, 1), :])
            p = jnp.where(hot, p - 2.0, p)
            acc = acc + jnp.sum(jnp.where(hot, v, 0.0).reshape(16, 8, 128), axis=0)
            p = p.astype(BF16)
            dl[r, c * 128:(c + 1) * 128] = p
            dlt[c * 128:(c + 1) * 128, r] = p.T
        pacc[...] += acc
        return carry

    lax.fori_loop(0, 8, dlogit, 0)

    sub = lax.broadcasted_iota(jnp.int32, (8, 128), 0)
    part = jnp.where(sub == me_row, row_lse, 0.0) + jnp.where(sub == y * 2 + k, cl_t[0:8, :], 0.0)
    loss_part = (part - 2.0 * pacc[...]) * LN2
    loss_now = {}

    def loss_begin(n, v, peers, slot, mine):
        lossbuf[slot + mine] = v
        cs = []
        for i, to in enumerate(peers):
            sem = slot + i
            dst = slot + (mine if len(peers) > 1 else 1)
            cs.append(rc(lossbuf.at[slot + mine], lossbuf.at[dst], ls.at[sem], lv.at[sem], to))
        for c in cs:
            c.start()
        loss_now[n] = cs

    def loss_end(n, slot, count):
        for c in loss_now[n]:
            c.wait()
        v = [lossbuf[slot + i] for i in range(count)]
        return v[0] + v[1] if count == 2 else (v[0] + v[1]) + (v[2] + v[3])

    zall, yall = [list(p.values()) for p in (zpeer, ypeer)]

    def grad_q(t):
        g = jnp.concatenate(
            [jnp.concatenate([gbuf[xj[t], m, i] for i in range(4)], axis=0) for m in range(2)],
            axis=1,
        )
        o = jnp.dot(dl[...], g, preferred_element_type=F32)
        for i in range(4):
            s_buf[i * 4 + t] = o[:, i * 128:(i + 1) * 128]

    def grad_g(t, rels, kk):
        cols = []
        for rel in rels:
            i = mod4(y + rel)
            j = jnp.where(i == x, 0, jnp.where(i == xo, 1, jnp.where(i == xi, 2, 3)))
            cols += [qbuf[2 * kk, j], qbuf[2 * kk + 1, j]]
        q = jnp.concatenate(cols, axis=1)
        return jnp.dot(dlt[t * 512:(t + 1) * 512, :], q, preferred_element_type=F32)

    sent = []

    class Side:
        def __init__(self, get, rows, bufs, sems, plus, minus, partner):
            self.get, self.rows, self.bufs, self.sems = get, rows, bufs, sems
            self.plus, self.minus, self.partner = plus, minus, partner
            self.msgs = {}

        def send(self, halves, slot, to):
            s, r, ss, sr = self.bufs
            cs, cv, vs, vv = self.sems
            src = slot
            if slot >= R4:
                src = slot - R4 + R1
                for c in self.msgs[src]:
                    c.wait_send()
                sent[:] = [c for c in sent if all(c is not d for d in self.msgs[src])]
            for n, v in enumerate(halves):
                code, sca = encode(v)
                s[src + n] = code
                ss[src + n] = sca
            here, there, n = pl.ds(src, len(halves)), pl.ds(slot, len(halves)), slot
            pair = (
                rc(s.at[here], r.at[there], cs.at[n], cv.at[n], to),
                rc(ss.at[here], sr.at[there], vs.at[n], vv.at[n], to),
            )
            for c in pair:
                c.start()
            sent.extend(pair)
            self.msgs[slot] = pair

        def arrive(self, slot):
            for c in self.msgs[slot]:
                c.wait_recv()

        def val(self, slot):
            return decode(self.bufs[1][slot], self.bufs[3][slot])

        def half(self, rel, t, u):
            return self.get(rel, t, pl.ds(u * self.rows, self.rows))

        def halves(self, rel, t):
            return [self.half(rel, t, u) for u in range(2)]

        def outer(self, t):
            n = (t - 2) * 2
            self.send(self.halves(2, t), R1 + n, self.partner)
            self.send(self.halves(1, t), R3P + n, self.plus)
            self.send(self.halves(3, t), R3M + n, self.minus)

        def inner(self, t):
            n = t * 2
            self.arrive(R1 + n)
            for u, to in ((0, self.plus), (1, self.minus)):
                self.send([self.half(2, t, u) + self.val(R1 + n + u)], R2 + n + u, to)
            self.send([self.half(1, t, 1)], R3PH + n + 1, self.plus)
            self.send([self.half(3, t, 0)], R3MH + n, self.minus)

        def late(self, t):
            n = t * 2
            self.arrive(R2 + n)
            self.send([self.half(1, t, 0) + self.val(R2 + n)], R3PH + n, self.plus)
            self.arrive(R2 + n + 1)
            self.send([self.half(3, t, 1) + self.val(R2 + n + 1)], R3MH + n + 1, self.minus)

        def across(self, t):
            n = (t - 2) * 2
            self.arrive(R3P + n)
            self.arrive(R3M + n)
            self.send(
                [self.half(0, t, u) + self.val(R3P + n + u) + self.val(R3M + n + u)
                 for u in range(2)],
                R4 + n, self.partner,
            )

        def final(self, t, u):
            n = t * 2
            if ("4", t) not in self.msgs:
                self.arrive(R4 + n)
                self.msgs["4", t] = True
            self.arrive(R3PH + n + u)
            self.arrive(R3MH + n + u)
            return (
                (self.half(0, t, u) + self.val(R4 + n + u))
                + (self.val(R3PH + n + u) + self.val(R3MH + n + u))
            )

    qside = Side(
        lambda rel, t, r: s_buf[mod4(z + rel) * 4 + t, r, :], 512,
        (qr_s, qr_r, qr_ss, qr_sr), (qcs, qcv, qss, qsv), zpeer[1], zpeer[3], part_q,
    )
    gside = Side(
        lambda rel, t, r: pg[rel, t, r, :], 256,
        (gr_s, gr_r, gr_ss, gr_sr), (gcs, gcv, gss, gsv), ypeer[1], ypeer[3], part_g,
    )
    order = (2, 1, 3, 0)
    xmsg = {}

    def grad_g_other(t):
        if t < 2:
            for c in xmsg[t + 2]:
                c.wait_send()
        o = grad_g(t, order, 1 - k)
        for n, rel in enumerate(order):
            code, sca = encode(o[:, n * 256:(n + 1) * 256])
            cx_s[t % 2, rel] = code
            cx_ss[t % 2, rel] = sca
        c1 = rc(cx_s.at[t % 2], cx_r.at[t], xs.at[t], xv.at[t], core)
        c2 = rc(cx_ss.at[t % 2], cx_sr.at[t], xss.at[t], xsv.at[t], core)
        c1.start()
        c2.start()
        xmsg[t] = (c1, c2)

    def grad_g_own(t):
        o = grad_g(t, order, k)
        for c in xmsg[t]:
            c.wait_recv()
        for n, rel in enumerate(order):
            pg[rel, t] = o[:, n * 256:(n + 1) * 256] + decode(cx_r[t, rel], cx_sr[t, rel])

    loss_begin(0, loss_part, [core], 0, 0)
    for t in (3, 2):
        grad_g_other(t)
        grad_q(t)
        qside.outer(t)
        grad_g_own(t)
        gside.outer(t)
    loss = loss_end(0, 0, 2)
    loss_begin(1, loss, [part_q], 2, 0)
    grad_g_other(1)
    grad_q(1)
    qside.inner(1)
    qside.across(3)
    loss = loss_end(1, 2, 2)
    loss_begin(2, loss, [part_g], 4, 0)
    grad_g_own(1)
    gside.inner(1)
    gside.across(3)
    loss = loss_end(2, 4, 2)
    loss_begin(3, loss, zall, 6, z)
    grad_g_other(0)
    grad_q(0)
    qside.inner(0)
    qside.late(1)
    loss = loss_end(3, 6, 4)
    loss_begin(4, loss, yall, 10, y)
    grad_g_own(0)
    gside.inner(0)
    gside.late(1)
    qside.across(2)
    gside.across(2)
    loss = loss_end(4, 10, 4)
    loss = jnp.sum(jnp.sum(loss, axis=0, keepdims=True), axis=1, keepdims=True)
    loss_ref[...] = jnp.broadcast_to(loss * (1.0 / 32768.0), (8, 128))
    qside.late(0)
    gside.late(0)
    for t in (1, 0):
        for c in xmsg[t]:
            c.wait_send()

    out_to = dev(xo, y, z, h)
    out_sem = k * 2
    for u in (1, 0):
        code, sca = encode(qside.final(1, u))
        qr_s[OUT + u] = code
        qr_ss[OUT + u] = sca
        for c in (
            rc(qr_s.at[OUT + u], qo_r.at[k, u], qcs.at[NSLOT + u], ov.at[out_sem + u], out_to),
            rc(qr_ss.at[OUT + u], qo_sr.at[k, u], qss.at[NSLOT + u], ovs.at[out_sem + u], out_to),
        ):
            c.start()
            sent.append(c)
    def put_g(n, v):
        r = pl.ds(n * 256, 256)
        gout[r, :] = v
        c = pltpu.make_async_copy(gout.at[r], gg_ref.at[r], osem.at[4 + n])
        c.start()
        return c

    puts = [put_g(2 + u, gside.final(1, u)) for u in (1, 0)]
    for u in (1, 0):
        qout[k, u] = qside.final(0, u)
    rows_k = pl.ds(k * 2, 2)
    out_core = rc(qout.at[k], qg_ref.at[rows_k], ms.at[7], mv.at[5 + k], core)
    out_here = pltpu.make_async_copy(qout.at[k], qg_ref.at[rows_k], osem.at[8])

    @pl.when(h == k)
    def _():
        out_here.start()

    @pl.when(h != k)
    def _():
        out_core.start()

    puts += [put_g(u, gside.final(0, u)) for u in (1, 0)]

    @pl.when(h == k)
    def _():
        out_here.wait()
        rc(qout.at[k], qg_ref.at[pl.ds((1 - k) * 2, 2)], ms.at[7], mv.at[6 - k], core).wait_recv()
        q1c.wait_send()

    @pl.when(h != k)
    def _():
        out_core.wait_send()
        moves = []
        for u in (1, 0):
            for kk in range(2):
                rc(qr_s.at[OUT], qo_r.at[kk, u], qcs.at[OUT], ov.at[kk * 2 + u],
                   out_to).wait_recv()
                rc(qr_ss.at[OUT], qo_sr.at[kk, u], qss.at[OUT], ovs.at[kk * 2 + u],
                   out_to).wait_recv()
                qout[kk, u] = decode(qo_r[kk, u], qo_sr[kk, u])
                c = pltpu.make_async_copy(
                    qout.at[kk, u], qg_ref.at[kk * 2 + u], osem.at[kk * 2 + u]
                )
                c.start()
                moves.append(c)
        for c in moves:
            c.wait()
        for c in q1o:
            c.wait_send()

    for c in puts:
        c.wait()
    pos_copy.wait_send()
    for m in (qm, gm):
        for c in m.values():
            c.wait_send()
    for c in ecopies + sent:
        c.wait_send()


def hand_on(loss_in, qg_in, gg_in, loss_out, qg_out, gg_out, qv, gv, sem):
    ins, outs = [], []
    for i in range(4):
        a, b = pl.ds(i * 512, 512), pl.ds(i * 256, 256)
        for n, (src, mid, dst, r) in enumerate(((qg_in, qv, qg_out, a), (gg_in, gv, gg_out, b))):
            ins.append(pltpu.make_async_copy(src.at[r], mid.at[r], sem.at[0, i, n]))
            outs.append(pltpu.make_async_copy(mid.at[r], dst.at[r], sem.at[1, i, n]))
    for c in ins:
        c.start()
    loss_out[0, 0] = loss_in[0, 0]
    for c, d in zip(ins, outs):
        c.wait()
        d.start()
    for c in outs:
        c.wait()


def on_device(query_embed, gist_embed, positive):
    pos = positive.reshape(16, 128)
    vm, dma = pltpu.VMEM, pltpu.SemaphoreType.DMA
    scratch = [
        vm((4, 4, 1024, 128), BF16),
        vm((4, 2, 4, 512, 256), BF16),
        vm((16, 1024, 128), F32),
        vm((1024, 2048), BF16),
        vm((2048, 1024), BF16),
        vm((2, 16, 128), jnp.int32),
        vm((8, 128), F32),
        vm((8, 128), F32),
        vm((16, 8, 128), F32),
        vm((16, 8, 128), F32),
        vm((8, 2, 8, 128), F32),
        vm((2, 2, 2, 8, 128), F32),
        vm((2, 4, 2, 2, 8, 128), F32),
        vm((16, 128), F32),
        vm((8, 128), F32),
        vm((OUT + 2, 512, 128), I16),
        vm((NSLOT, 512, 128), I16),
        vm((OUT + 2, 8, 128), F32),
        vm((NSLOT, 8, 128), F32),
        vm((OUT, 256, 256), I16),
        vm((NSLOT, 256, 256), I16),
        vm((OUT, 8, 256), F32),
        vm((NSLOT, 8, 256), F32),
        vm((2, 4, 512, 256), I16),
        vm((4, 4, 512, 256), I16),
        vm((2, 4, 8, 256), F32),
        vm((4, 4, 8, 256), F32),
        vm((4, 4, 512, 256), F32),
        vm((2, 2, 512, 128), F32),
        vm((1024, 256), F32),
        vm((2, 2, 512, 128), I16),
        vm((2, 2, 8, 128), F32),
        vm((14, 8, 128), F32),
        dma((NGATHER,)), dma((NGATHER,)),
        dma((NGATHER,)), dma((NGATHER,)),
        dma((4, 4, 2)), dma((4, 4, 2)),
        dma((8,)), dma((8,)),
        dma((7,)), dma((7,)),
        dma((7,)), dma((7,)),
        dma((14,)), dma((14,)),
        dma((NSLOT + 2,)), dma((NSLOT,)),
        dma((NSLOT + 2,)), dma((NSLOT,)),
        dma((NSLOT,)), dma((NSLOT,)),
        dma((NSLOT,)), dma((NSLOT,)),
        dma((4,)), dma((4,)),
        dma((4,)), dma((4,)),
        dma((4,)), dma((4,)),
        dma((4,)),
        dma((9,)),
    ]
    loss, qg, gg = pl.pallas_call(
        kernel,
        out_shape=[
            jax.ShapeDtypeStruct((8, 128), F32),
            jax.ShapeDtypeStruct((4, 512, 128), F32),
            jax.ShapeDtypeStruct((1024, 256), F32),
        ],
        in_specs=[
            pl.BlockSpec(memory_space=pl.ANY),
            pl.BlockSpec(memory_space=pl.ANY),
            pl.BlockSpec(memory_space=pltpu.VMEM),
        ],
        out_specs=[
            pl.BlockSpec(memory_space=pltpu.VMEM),
            pl.BlockSpec(memory_space=pl.ANY),
            pl.BlockSpec(memory_space=pl.ANY),
        ],
        scratch_shapes=scratch,
        compiler_params=pltpu.CompilerParams(
            collective_id=0, has_side_effects=True, vmem_limit_bytes=63 * 2**20
        ),
    )(query_embed, gist_embed, pos)
    loss, qg, gg = pl.pallas_call(
        hand_on,
        out_shape=[
            jax.ShapeDtypeStruct((1, 1), F32),
            jax.ShapeDtypeStruct((2048, 128), F32),
            jax.ShapeDtypeStruct((1024, 256), F32),
        ],
        in_specs=[
            pl.BlockSpec(memory_space=pltpu.VMEM),
            pl.BlockSpec(memory_space=pl.ANY),
            pl.BlockSpec(memory_space=pl.ANY),
        ],
        out_specs=[
            pl.BlockSpec(memory_space=pltpu.SMEM),
            pl.BlockSpec(memory_space=pl.ANY),
            pl.BlockSpec(memory_space=pl.ANY),
        ],
        scratch_shapes=[vm((2048, 128), F32), vm((1024, 256), F32), dma((2, 4, 2))],
    )(loss, qg.reshape(2048, 128), gg)
    return loss[0, 0], qg, gg


def solution(mesh):
    in_specs = (P("row", "col"), P("col", "row"), P("row"))
    out_specs = (P(), P("row", "col"), P("col", "row"))
    return jax.shard_map(
        on_device, mesh=mesh, in_specs=in_specs, out_specs=out_specs, check_vma=False
    )
```

time: 151 us -> 117 us (0.77)
  Pallas kernels: 146 us -> 116 us
  local copies, waits for them, and re-layouts: 4.52 us -> 0 us
    pallas_call x1, Pallas kernels: 146 us -> 112 us  [on_device(): pl.pallas_call(kernel, out_shape=[jax.ShapeDtypeStruct((8, 128), F32), ja...]
    pallas_call x0 -> x1, Pallas kernels: none -> 3.59 us  [on_device(): pl.pallas_call(hand_on, out_shape=[jax.ShapeDtypeStruct((1, 1), F32), jax...]
    unnamed x4 -> x0, local copies, waits for them, and re-layouts: 3.32 us -> none
where the time goes in v2:
time: 117 us
  Pallas kernels  116 us (99%)
    pallas_call x1, Pallas kernels, on_device(): pl.pallas_call(kernel, out_shape=[jax.ShapeDtypeStruct((8, 128), F32), ja...  112 us
    pallas_call x1, Pallas kernels, on_device(): pl.pallas_call(hand_on, out_shape=[jax.ShapeDtypeStruct((1, 1), F32), jax...  3.59 us

profile of v2, /device:TPU:1, one launch (start us, length us, event | category | flops | bytes accessed | tf_op | source)
XLA Modules:
  0.0 116.6 jit_solution(11519275472631912628)
XLA Ops:
  0.6 112.2 %shard_map.58 = (f32[8,128]{1,0:T(8,128)}, f32[4,512,128]{2,1,0:T(8,128)}, f32[1024,256]{1,0:T(8,128)}) custom-call(bf16[2048,128]{1,0:T(8,128)(2,1)} %q_ref.1, bf16[1024,256]{1,0:T(8,128)(2,1)} %g_ref.1, s32[16,128]{1,0:T(8,128)} %bitcast.4), custom_call_target="tpu_custom_call" | custom-call | tf_op jit(solution)/shard_map/pallas_call | solution.py:735
  112.8 3.6 %shard_map.59 = (f32[1,1]{1,0:T(1,128)}, f32[2048,128]{1,0:T(8,128)}, f32[1024,256]{1,0:T(8,128)}) custom-call(f32[8,128]{1,0:T(8,128)} %get-tuple-element.9.loss_in, f32[2048,128]{1,0:T(8,128)} %bitcast.3, f32[1024,256]{1,0:T(8,128)} %get-tuple-element.11.gg_in), custom_call_target="tpu_custom_call" | custom-call | tf_op jit(solution)/shard_map/pallas_call | solution.py:757

commit v3 on v2

v3 whole, which is shorter than its diff:
```python
import functools
import math

import jax
import jax.numpy as jnp
from jax import lax
from jax.experimental import pallas as pl
from jax.experimental.pallas import tpu as pltpu
from jax.sharding import PartitionSpec as P

D = 2048
MESH = pl.DeviceIdType.MESH
LOG2E = 1.4426950408889634
LN2 = 0.6931471805599453
F32 = jnp.float32
BF16 = jnp.bfloat16
I16 = jnp.int16
TOP = 14.98

A, BP, BM, C, DD = 0, 4, 12, 20, 24
R1, R3P, R3M, R2, R3PH, R3MH, R4, NSLOT = 0, 4, 8, 12, 16, 20, 24, 28
OUT = R4


def where_am_i():
    row = lax.axis_index("row")
    col = lax.axis_index("col")
    return lax.div(col, 4), lax.div(row, 2), lax.rem(col, 4), lax.rem(row, 2)


def mod4(v):
    return lax.rem(v + 8, 4)


def encode(x):
    rows, cols = x.shape
    x3 = x.reshape(rows // 8, 8, cols)
    top = jnp.maximum(jnp.max(jnp.abs(x3), axis=0), 1e-30)
    e = jnp.ceil(jnp.log2(top) * 64.0)
    code = jnp.round(x3 * jnp.exp2(TOP - e * (1.0 / 64.0))[None]).reshape(rows, cols)
    return code.astype(jnp.int32).astype(I16), jnp.concatenate([e, e]).astype(jnp.int32).astype(I16)


def put(ref, v):
    rows = v.shape[0]
    code, e = encode(v)
    ref[pl.ds(0, rows), :] = code
    ref[pl.ds(rows, 16), :] = e


def decode(ref, rows):
    e = ref[pl.ds(rows, 16), :].astype(jnp.int32).astype(F32)[:8]
    x = ref[pl.ds(0, rows), :].astype(jnp.int32).astype(F32)
    x3 = x.reshape(rows // 8, 8, x.shape[1]) * jnp.exp2(e * (1.0 / 64.0) - TOP)[None]
    return x3.reshape(x.shape)


def kernel(
    q_ref, g_ref, pos_ref, loss_ref, qg_ref, gg_ref,
    qbuf, gbuf, s_buf, dl, dlt, posbuf,
    ml, sl, mc, sc, rowst, colst0, colst, cl_t, pacc,
    qr_s, qr_r, gr_s, gr_r, cx_s, cx_r, pg, qout, qo_r, lossbuf,
    qs, qv, gs, gv, es, ev, ms, mv, rs, rv, cs_, cv_, ls, lv, xs, xv, ov, lsem, osem,
):
    x, y, z, k = where_am_i()
    h = lax.div(x, 2)
    e = lax.rem(x, 2)
    xi = x + 1 - 2 * e
    xo = 3 - x
    xio = 3 - xi
    xj = [x, xo, xi, xio]

    def dev(xx, yy, zz, kk):
        return (yy * 2 + kk, xx * 4 + zz)

    core = dev(x, y, z, 1 - k)
    part_q = dev(xi, y, z, k)
    part_g = dev(xo, y, z, k)
    part_g2 = dev(xo, y, z, 1 - k)
    zpeer = {d: dev(x, y, mod4(z + d), k) for d in (1, 2, 3)}
    ypeer = {d: dev(x, mod4(y + d), z, k) for d in (1, 2, 3)}
    zipeer = {d: dev(xi, y, mod4(z + d), k) for d in (1, 2, 3)}
    yopeer = {d: dev(xo, mod4(y + d), z, k) for d in (1, 2, 3)}
    everyone = [core, part_q, part_g, part_g2]
    for group in (zpeer, ypeer, zipeer, yopeer):
        everyone += list(group.values())

    barrier = pltpu.get_barrier_semaphore()
    for other in everyone:
        pl.semaphore_signal(barrier, inc=1, device_id=other, device_id_type=MESH)

    def rc(src, dst, s, v, to):
        return pltpu.make_async_remote_copy(
            src_ref=src, dst_ref=dst, send_sem=s, recv_sem=v, device_id=to, device_id_type=MESH
        )

    gl = [
        pltpu.make_async_copy(g_ref.at[pl.ds(t * 512, 512)], gbuf.at[y, k, t], lsem.at[t])
        for t in range(2)
    ]
    for c in gl:
        c.start()
    here = pltpu.make_async_copy(q_ref.at[pl.ds(k * 1024, 1024)], qbuf.at[z, 0], lsem.at[2])
    posc = pltpu.make_async_copy(pos_ref, posbuf.at[k], lsem.at[3])
    posc.start()

    @pl.when(h == k)
    def _():
        here.start()

    pl.semaphore_wait(barrier, len(everyone))

    pos_copy = rc(pos_ref, posbuf.at[k], ms.at[0], mv.at[0], core)
    pos_copy.start()
    q1c = rc(q_ref.at[pl.ds((1 - k) * 1024, 1024)], qbuf.at[z, 0], ms.at[1], mv.at[1], core)
    q1o = [
        rc(q_ref.at[pl.ds(kk * 1024 + u * 512, 512)], qbuf.at[z, 1, pl.ds(u * 512, 512)],
           ms.at[2], mv.at[2 + u], dev(xo, y, z, kk))
        for u in range(2) for kk in range(2)
    ]

    @pl.when(h == k)
    def _():
        q1c.start()

    @pl.when(h != k)
    def _():
        for c in q1o:
            c.start()

    def qp(i, t, u):
        return qbuf.at[i, t, pl.ds(u * 512, 512)]

    def gp(i, t, u):
        return gbuf.at[i, k, t, pl.ds(u * 256, 256)]

    def ring(buf, r, sems, semv, plus, minus, partner):
        def msg(i, t, u, t2, idx, to):
            return rc(buf(i, t, u), buf(i, t2, u), sems.at[0], semv.at[idx], to)

        before, after, far = mod4(r - 1), mod4(r + 1), mod4(r + 2)
        m = {}
        for t in range(4):
            for u in range(2):
                n = t * 2 + u
                if t < 2:
                    m["a", t, u] = msg(r, t, u, t + 2, A + n, partner)
                    m["d", t, u] = msg(far, t, u, t + 2, DD + n, partner)
                    m["c", t, u] = msg(before if u == 0 else after, t, u, t, C + n,
                                       plus if u == 0 else minus)
                m["p", t, u] = msg(r, t, u, t, BP + n, plus)
                m["m", t, u] = msg(r, t, u, t, BM + n, minus)
        return m

    qm = ring(qp, z, qs, qv, zpeer[1], zpeer[3], part_q)
    gm = ring(gp, y, gs, gv, ypeer[1], ypeer[3], part_g)
    yb, ya, yf = mod4(y - 1), mod4(y + 1), mod4(y + 2)

    def start_core(i, t, u):
        rc(gp(i, t, u), gp(i, t, u), es.at[max(t - 1, 0)], ev.at[max(t - 1, 0)], core).start()

    def both(m, t, first):
        u = first
        m["p", t, u].start()
        m["m", t, 1 - u].start()

    def on(m, t):
        m["p", t, 0].wait_recv()
        m["c", t, 0].start()
        m["m", t, 1].wait_recv()
        m["c", t, 1].start()

    for c in gl:
        c.wait()
    both(gm, 0, 0)
    both(gm, 0, 1)
    for t in range(2):
        for u in range(2):
            gm["a", t, u].start()
    both(gm, 1, 0)

    @pl.when(h == k)
    def _():
        here.wait()

    @pl.when(h != k)
    def _():
        q1c.wait_recv()

    both(qm, 0, 0)
    both(qm, 0, 1)
    for u in range(2):
        qm["a", 0, u].start()
    for t in range(2):
        for u in range(2):
            start_core(y, t, u)
    on(gm, 0)
    on(qm, 0)
    both(gm, 1, 1)
    q1o[0].wait_recv()
    q1o[2].wait_recv()
    both(qm, 1, 0)
    qm["a", 1, 0].start()
    both(qm, 1, 1)
    qm["a", 1, 1].start()
    start_core(yb, 0, 0)
    start_core(ya, 0, 1)
    gm["p", 0, 1].wait_recv()
    start_core(yb, 0, 1)
    gm["m", 0, 0].wait_recv()
    start_core(ya, 0, 0)
    on(gm, 1)
    start_core(yb, 1, 0)
    start_core(ya, 1, 1)
    for u in range(2):
        gm["c", 0, u].wait_recv()
        gm["d", 0, u].start()
        start_core(yf, 0, u)
        qm["c", 0, u].wait_recv()
        qm["d", 0, u].start()
    on(qm, 1)
    for u in range(2):
        gm["a", 0, u].wait_recv()
        gm["p", 2, u].start()
        gm["m", 2, u].start()
        start_core(y, 2, u)
        qm["a", 0, u].wait_recv()
        qm["p", 2, u].start()
        qm["m", 2, u].start()
    gm["p", 1, 1].wait_recv()
    start_core(yb, 1, 1)
    gm["m", 1, 0].wait_recv()
    start_core(ya, 1, 0)
    for u in range(2):
        qm["a", 1, u].wait_recv()
        qm["p", 3, u].start()
        qm["m", 3, u].start()
        gm["a", 1, u].wait_recv()
        gm["p", 3, u].start()
        gm["m", 3, u].start()
        start_core(y, 3, u)
    for u in range(2):
        gm["c", 1, u].wait_recv()
        gm["d", 1, u].start()
        start_core(yf, 1, u)
        qm["c", 1, u].wait_recv()
        qm["d", 1, u].start()
    def all_core(n, mine):
        r = gbuf.at[:, mine, pl.ds(0, 2) if n == 0 else pl.ds(n + 1, 1)]
        return rc(r, r, es.at[n], ev.at[n], core)

    scale = LOG2E / math.sqrt(D)

    def logits(t, js, add):
        g = jnp.concatenate([gbuf[xj[j], m, t] for j in js for m in range(2)], axis=1)
        q = jnp.concatenate(
            [qbuf[2 * m + u, j] for j in js for m in range(2) for u in range(2)], axis=1
        )
        s = lax.dot_general(q, g, (((1,), (1,)), ((), ())), preferred_element_type=F32)
        s = s * scale
        for u in range(4):
            v = s[:, u * 128:(u + 1) * 128]
            s_buf[t * 4 + u] = s_buf[t * 4 + u] + v if add else v

    def queries_there(t):
        for u in range(2):
            if t >= 2 or u == 1:
                qm["p", t, u].wait_recv()
            if t >= 2 or u == 0:
                qm["m", t, u].wait_recv()
            if t >= 2:
                qm["d", t - 2, u].wait_recv()

    queries_there(0)
    queries_there(1)
    all_core(0, 1 - k).wait_recv()
    logits(0, (0, 1), False)
    logits(1, (0, 1), False)
    for t in range(2, 4):
        for u in range(2):
            gm["p", t, u].wait_recv()
            start_core(yb, t, u)
            gm["m", t, u].wait_recv()
            start_core(ya, t, u)
        if t == 2:
            for u in range(2):
                gm["d", 0, u].wait_recv()
                start_core(yf, 2, u)
            queries_there(2)
            all_core(1, 1 - k).wait_recv()
            logits(0, (2,), True)
            logits(1, (2,), True)
            logits(2, (0, 1, 2), False)
    for u in range(2):
        gm["d", 1, u].wait_recv()
        start_core(yf, 3, u)
    queries_there(3)
    posc.wait()
    pos_copy.wait_recv()

    def stats(t):
        for u in range(4):
            c = t * 4 + u
            v3 = s_buf[c].reshape(128, 8, 128)
            top = jnp.max(v3, axis=0)
            mc[c] = top
            sc[c] = jnp.sum(jnp.exp2(v3 - top[None]), axis=0)
        for b in range(2):
            for d in range(4):
                r, rb = pl.ds(b * 512 + d * 128, 128), pl.ds(d * 128, 128)
                v = [s_buf[t * 4 + u, r, :] for u in range(4)]
                top = jnp.maximum(jnp.maximum(v[0], v[1]), jnp.maximum(v[2], v[3]))
                if t > 0:
                    old = qout[0, b, rb, :]
                    top = jnp.maximum(old, top)
                e = [jnp.exp2(w - top) for w in v]
                total = (e[0] + e[1]) + (e[2] + e[3])
                if t > 0:
                    total = total + qout[1, b, rb, :] * jnp.exp2(old - top)
                qout[0, b, rb, :] = top
                qout[1, b, rb, :] = total

    for t in range(3):
        logits(t, (3,), True)
        if t > 0:
            stats(t - 1)
    all_core(2, 1 - k).wait_recv()
    logits(3, (0, 1, 2, 3), False)
    stats(2)
    stats(3)
    for a in range(8):
        rb = pl.ds((a % 4) * 128, 128)
        tt = qout[0, a // 4, rb, :].T
        peak = jnp.max(tt, axis=0, keepdims=True)
        total = qout[1, a // 4, rb, :].T
        ml[pl.ds(a, 1), :] = peak
        sl[pl.ds(a, 1), :] = jnp.sum(total * jnp.exp2(tt - peak), axis=0, keepdims=True)

    for c in range(16):
        peak = jnp.max(mc[c], axis=0, keepdims=True)
        one = jnp.sum(sc[c] * jnp.exp2(mc[c] - peak), axis=0, keepdims=True)
        colst0[0, c // 8, 0, pl.ds(c % 8, 1), :] = peak
        colst0[0, c // 8, 1, pl.ds(c % 8, 1), :] = one
    ccopy = rc(colst0.at[0], colst0.at[1], ms.at[3], mv.at[4], core)
    ccopy.start()

    me_row = e * 4 + z
    rowst[me_row, 0] = ml[...]
    rowst[me_row, 1] = sl[...]
    for to in list(zpeer.values()) + list(zipeer.values()) + [part_q]:
        rc(rowst.at[me_row], rowst.at[me_row], rs, rv, to).start()
    rall = rc(rowst.at[pl.ds(0, 7)], rowst.at[pl.ds(0, 7)], rs, rv, part_q)

    ccopy.wait()
    for i in range(2):
        m0, m1 = colst0[0, i, 0], colst0[1, i, 0]
        peak = jnp.maximum(m0, m1)
        colst[y, i, 0] = peak
        colst[y, i, 1] = colst0[0, i, 1] * jnp.exp2(m0 - peak) + colst0[1, i, 1] * jnp.exp2(
            m1 - peak
        )
    for to in ypeer.values():
        rc(colst.at[y], colst.at[y], cs_, cv_, to).start()
    for to in list(yopeer.values()) + [part_g]:
        rc(colst.at[y], colst.at[4 + y], cs_, cv_, to).start()
    kall = rc(colst.at[pl.ds(0, 7)], colst.at[pl.ds(0, 7)], cs_, cv_, part_g)

    rall.wait()
    peak = rowst[0, 0]
    for n in range(1, 8):
        peak = jnp.maximum(peak, rowst[n, 0])
    tot = jnp.zeros_like(peak)
    for n in range(8):
        tot = tot + rowst[n, 1] * jnp.exp2(rowst[n, 0] - peak)
    row_lse = peak + jnp.log2(tot)
    ml[...] = row_lse

    kall.wait()
    for i in range(2):
        peak = colst[0, i, 0]
        for n in range(4):
            peak = jnp.maximum(jnp.maximum(peak, colst[n, i, 0]), colst[4 + n, 1 - i, 0])
        tot = jnp.zeros_like(peak)
        for n in range(4):
            a0 = colst[n, i, 1] * jnp.exp2(colst[n, i, 0] - peak)
            a1 = colst[4 + n, 1 - i, 1] * jnp.exp2(colst[4 + n, 1 - i, 0] - peak)
            tot = tot + (a0 + a1)
        cl_t[pl.ds(i * 8, 8), :] = peak + jnp.log2(tot)

    for a in range(8):
        r = pl.ds((a % 4) * 128, 128)
        qout[0, a // 4, r, :] = jnp.broadcast_to(ml[pl.ds(a, 1), :], (128, 128)).T
        pos = posbuf[h, pl.ds(k * 8 + a, 1), :].astype(F32)
        qout[1, a // 4, r, :] = jnp.broadcast_to(pos, (128, 128)).T
    lane = lax.broadcasted_iota(jnp.int32, (1, 128), 1)
    first = [(x * 4 + z) * 1024, (xo * 4 + z) * 1024]

    def dlogit(t):
        acc = jnp.zeros((8, 128), F32)
        for u in range(4):
            c = t * 4 + u
            cl = cl_t[pl.ds(c, 1), :]
            own = (lane + (first[c // 8] + (c % 8) * 128)).astype(F32)
            for a in range(8):
                r, rb = pl.ds(a * 128, 128), pl.ds((a % 4) * 128, 128)
                v = s_buf[c, r, :]
                hot = jnp.where(qout[1, a // 4, rb, :] == own, 2.0, 0.0)
                p = jnp.exp2(v - qout[0, a // 4, rb, :]) + jnp.exp2(v - cl) - hot
                acc = acc + jnp.sum((v * hot).reshape(16, 8, 128), axis=0)
                p = p.astype(BF16)
                dl[r, c * 128:(c + 1) * 128] = p
                dlt[c * 128:(c + 1) * 128, r] = p.T
        pacc[t] = acc

    dlogit(3)

    sub = lax.broadcasted_iota(jnp.int32, (8, 128), 0)
    lse_part = jnp.where(sub == me_row, row_lse, 0.0) + jnp.where(sub == y * 2 + k, cl_t[0:8, :], 0.0)
    loss_now = {}

    def loss_begin(n, v, peers, slot, mine):
        lossbuf[slot + mine] = v
        dst = slot + (mine if len(peers) > 1 else 1)
        for to in peers:
            rc(lossbuf.at[slot + mine], lossbuf.at[dst], ls.at[n], lv.at[n], to).start()
        got = lossbuf.at[pl.ds(slot, len(peers))]
        loss_now[n] = rc(got, got, ls.at[n], lv.at[n], peers[0])

    def loss_end(n, slot, count):
        loss_now[n].wait()
        v = [lossbuf[slot + i] for i in range(count)]
        return v[0] + v[1] if count == 2 else (v[0] + v[1]) + (v[2] + v[3])

    zall, yall = [list(p.values()) for p in (zpeer, ypeer)]

    def grad_q(t):
        g = jnp.concatenate(
            [jnp.concatenate([gbuf[xj[t], m, i] for i in range(4)], axis=0) for m in range(2)],
            axis=1,
        )
        o = jnp.dot(dl[...], g, preferred_element_type=F32)
        for i in range(4):
            s_buf[i * 4 + t] = o[:, i * 128:(i + 1) * 128]

    def grad_g(t, rels, kk):
        cols = []
        for rel in rels:
            i = mod4(y + rel)
            j = jnp.where(i == x, 0, jnp.where(i == xo, 1, jnp.where(i == xi, 2, 3)))
            cols += [qbuf[2 * kk, j], qbuf[2 * kk + 1, j]]
        q = jnp.concatenate(cols, axis=1)
        return jnp.dot(dlt[t * 512:(t + 1) * 512, :], q, preferred_element_type=F32)

    for m, sem, ref in ((qm, qs, qbuf.at[:, :, pl.ds(0, 896)]),
                        (gm, gs, gbuf.at[:, k, :, pl.ds(0, 448)])):
        rc(ref, ref, sem.at[0], qv.at[0], core).wait_send()
    for n in range(3):
        all_core(n, k).wait_send()

    class Side:
        def __init__(self, get, rows, bufs, sems, plus, minus, partner):
            self.get, self.rows, self.bufs, self.sems = get, rows, bufs, sems
            self.plus, self.minus, self.partner = plus, minus, partner
            self.msgs = {}

        def send(self, *many):
            s, r = self.bufs
            cs, cv = self.sems
            copies = []
            for halves, slot, to in many:
                src, sem = slot, 1
                if slot >= R4:
                    src = slot - R4 + R1
                    self.msgs[src].wait_send()
                elif slot < R3P:
                    sem = 2 + (slot - R1) // 2
                here, there = pl.ds(src, len(halves)), pl.ds(slot, len(halves))
                c = rc(s.at[here], r.at[there], cs.at[sem], cv.at[slot], to)
                self.msgs[slot] = c
                copies.append(c)
                for n, v in enumerate(halves):
                    put(s.at[src + n], v)
            for c in copies:
                c.start()

        def sent(self, count):
            r = self.bufs[1].at[pl.ds(0, count)]
            rc(r, r, self.sems[0].at[1], self.sems[1].at[0], self.plus).wait_send()

        def arrive(self, slot):
            self.msgs[slot].wait_recv()

        def val(self, slot):
            return decode(self.bufs[1].at[slot], self.rows)

        def half(self, rel, t, u):
            return self.get(rel, t, pl.ds(u * self.rows, self.rows))

        def halves(self, rel, t):
            return [self.half(rel, t, u) for u in range(2)]

        def outer(self, t):
            n = (t - 2) * 2
            self.send(
                (self.halves(2, t), R1 + n, self.partner),
                (self.halves(1, t), R3P + n, self.plus),
                (self.halves(3, t), R3M + n, self.minus),
            )

        def inner(self, t):
            n = t * 2
            self.arrive(R1 + n)
            far = [self.half(2, t, u) + self.val(R1 + n + u) for u in range(2)]
            self.send(
                ([far[0]], R2 + n, self.plus),
                ([far[1]], R2 + n + 1, self.minus),
                ([self.half(1, t, 1)], R3PH + n + 1, self.plus),
                ([self.half(3, t, 0)], R3MH + n, self.minus),
            )

        def late(self, t):
            n = t * 2
            self.arrive(R2 + n)
            self.arrive(R2 + n + 1)
            self.send(
                ([self.half(1, t, 0) + self.val(R2 + n)], R3PH + n, self.plus),
                ([self.half(3, t, 1) + self.val(R2 + n + 1)], R3MH + n + 1, self.minus),
            )

        def across(self, t):
            n = (t - 2) * 2
            self.arrive(R3P + n)
            self.arrive(R3M + n)
            v = [
                self.half(0, t, u) + self.val(R3P + n + u) + self.val(R3M + n + u)
                for u in range(2)
            ]
            self.send((v, R4 + n, self.partner))

        def final(self, t, u):
            n = t * 2
            if ("4", t) not in self.msgs:
                self.arrive(R4 + n)
                self.msgs["4", t] = True
            self.arrive(R3PH + n + u)
            self.arrive(R3MH + n + u)
            return (
                (self.half(0, t, u) + self.val(R4 + n + u))
                + (self.val(R3PH + n + u) + self.val(R3MH + n + u))
            )

    qside = Side(
        lambda rel, t, r: s_buf[mod4(z + rel) * 4 + t, r, :], 512,
        (qr_s, qr_r), (qs, qv), zpeer[1], zpeer[3], part_q,
    )
    gside = Side(
        lambda rel, t, r: pg[rel, t, r, :], 256,
        (gr_s, gr_r), (gs, gv), ypeer[1], ypeer[3], part_g,
    )
    order = (2, 1, 3, 0)
    xmsg = {}

    def grad_g_other(t, beside=None, *args):
        if t < 2:
            xmsg[t + 2].wait_send()
        o = grad_g(t, order, 1 - k)
        if beside is not None:
            beside(*args)
        for n, rel in enumerate(order):
            put(cx_s.at[t % 2, rel], o[:, n * 256:(n + 1) * 256])
        xmsg[t] = rc(cx_s.at[t % 2], cx_r.at[t], xs.at[t % 2], xv.at[t], core)
        xmsg[t].start()

    def grad_g_own(t):
        o = grad_g(t, order, k)
        for n, rel in enumerate(order):
            pg[rel, t] = o[:, n * 256:(n + 1) * 256]

    def grad_g_sum(t):
        xmsg[t].wait_recv()
        for rel in order:
            pg[rel, t] += decode(cx_r.at[t, rel], 512)

    grad_g_other(3, dlogit, 0)
    grad_g_own(3)
    dlogit(1)
    dlogit(2)
    grad_q(3)
    qside.outer(3)
    grad_g_sum(3)
    gside.outer(3)
    hits = (pacc[0] + pacc[1]) + (pacc[2] + pacc[3])
    loss_begin(0, (lse_part - hits) * LN2, [core], 0, 0)
    grad_g_other(2)
    grad_q(2)
    qside.outer(2)
    grad_g_own(2)
    grad_g_sum(2)
    gside.outer(2)
    loss = loss_end(0, 0, 2)
    loss_begin(1, loss, [part_q], 2, 0)
    grad_g_other(1)
    grad_q(1)
    qside.inner(1)
    qside.across(3)
    loss = loss_end(1, 2, 2)
    loss_begin(2, loss, [part_g], 4, 0)
    grad_g_own(1)
    grad_g_sum(1)
    gside.inner(1)
    gside.across(3)
    loss = loss_end(2, 4, 2)
    loss_begin(3, loss, zall, 6, z)
    grad_g_other(0)
    grad_q(0)
    qside.inner(0)
    qside.late(1)
    loss = loss_end(3, 6, 4)
    loss_begin(4, loss, yall, 10, y)
    grad_g_own(0)
    grad_g_sum(0)
    gside.inner(0)
    gside.late(1)
    qside.across(2)
    gside.across(2)
    loss = loss_end(4, 10, 4)
    loss = jnp.sum(jnp.sum(loss, axis=0, keepdims=True), axis=1, keepdims=True)
    loss_ref[...] = jnp.broadcast_to(loss * (1.0 / 32768.0), (8, 128))
    qside.late(0)
    gside.late(0)
    for t in (1, 0):
        xmsg[t].wait_send()

    out_to = dev(xo, y, z, h)
    out_sem = k * 2
    for u in (1, 0):
        put(qr_s.at[OUT + u], qside.final(1, u))
        rc(qr_s.at[OUT + u], qo_r.at[k, u], qs.at[1], ov.at[out_sem + u], out_to).start()

    def put_g(t, u):
        r = pl.ds(u * 256, 256)
        pg[0, t, r, :] = gside.final(t, u)
        n = t * 2 + u
        c = pltpu.make_async_copy(pg.at[0, t, r], gg_ref.at[pl.ds(n * 256, 256)], osem.at[4 + n])
        c.start()
        return c

    puts = [put_g(1, u) for u in (1, 0)]
    for u in (1, 0):
        qout[k, u] = qside.final(0, u)
    rows_k = pl.ds(k * 2, 2)
    out_core = rc(qout.at[k], qg_ref.at[rows_k], ms.at[4], mv.at[5 + k], core)
    out_here = pltpu.make_async_copy(qout.at[k], qg_ref.at[rows_k], osem.at[8])

    @pl.when(h == k)
    def _():
        out_here.start()

    @pl.when(h != k)
    def _():
        out_core.start()

    puts += [put_g(0, u) for u in (1, 0)]

    @pl.when(h == k)
    def _():
        out_here.wait()
        rc(qout.at[k], qg_ref.at[pl.ds((1 - k) * 2, 2)], ms.at[4], mv.at[6 - k], core).wait_recv()
        q1c.wait_send()

    @pl.when(h != k)
    def _():
        out_core.wait_send()
        moves = []
        for u in (1, 0):
            for kk in range(2):
                rc(qr_s.at[OUT], qo_r.at[kk, u], qs.at[1], ov.at[kk * 2 + u],
                   out_to).wait_recv()
                qout[kk, u] = decode(qo_r.at[kk, u], 512)
                c = pltpu.make_async_copy(
                    qout.at[kk, u], qg_ref.at[kk * 2 + u], osem.at[kk * 2 + u]
                )
                c.start()
                moves.append(c)
        for c in moves:
            c.wait()
        rc(q_ref, q_ref, ms.at[2], mv.at[2], core).wait_send()

    for c in puts:
        c.wait()
    pos_copy.wait_send()
    qside.sent(OUT + 2)
    gside.sent(OUT)


def hand_on(loss_in, qg_in, gg_in, loss_out, qg_out, gg_out, qv, gv, sem):
    ins, outs = [], []
    for i in range(4):
        a, b = pl.ds(i * 512, 512), pl.ds(i * 256, 256)
        for n, (src, mid, dst, r) in enumerate(((qg_in, qv, qg_out, a), (gg_in, gv, gg_out, b))):
            ins.append(pltpu.make_async_copy(src.at[r], mid.at[r], sem.at[0, i, n]))
            outs.append(pltpu.make_async_copy(mid.at[r], dst.at[r], sem.at[1, i, n]))
    for c in ins:
        c.start()
    loss_out[0, 0] = loss_in[0, 0]
    for c, d in zip(ins, outs):
        c.wait()
        d.start()
    for c in outs:
        c.wait()


def on_device(query_embed, gist_embed, positive):
    pos = positive.reshape(16, 128)
    vm, dma = pltpu.VMEM, pltpu.SemaphoreType.DMA
    scratch = [
        vm((4, 4, 1024, 128), BF16),
        vm((4, 2, 4, 512, 256), BF16),
        vm((16, 1024, 128), F32),
        vm((1024, 2048), BF16),
        vm((2048, 1024), BF16),
        vm((2, 16, 128), jnp.int32),
        vm((8, 128), F32),
        vm((8, 128), F32),
        vm((16, 8, 128), F32),
        vm((16, 8, 128), F32),
        vm((8, 2, 8, 128), F32),
        vm((2, 2, 2, 8, 128), F32),
        vm((8, 2, 2, 8, 128), F32),
        vm((16, 128), F32),
        vm((4, 8, 128), F32),
        vm((OUT + 2, 528, 128), I16),
        vm((NSLOT, 528, 128), I16),
        vm((OUT, 272, 256), I16),
        vm((NSLOT, 272, 256), I16),
        vm((2, 4, 528, 256), I16),
        vm((4, 4, 528, 256), I16),
        vm((4, 4, 512, 256), F32),
        vm((2, 2, 512, 128), F32),
        vm((2, 2, 528, 128), I16),
        vm((14, 8, 128), F32),
        dma((4,)), dma((NSLOT,)),
        dma((4,)), dma((NSLOT,)),
        dma((3,)), dma((3,)),
        dma((5,)), dma((7,)),
        dma, dma,
        dma, dma,
        dma((5,)), dma((5,)),
        dma((2,)), dma((4,)),
        dma((4,)),
        dma((4,)),
        dma((9,)),
    ]
    loss, qg, gg = pl.pallas_call(
        kernel,
        out_shape=[
            jax.ShapeDtypeStruct((8, 128), F32),
            jax.ShapeDtypeStruct((4, 512, 128), F32),
            jax.ShapeDtypeStruct((1024, 256), F32),
        ],
        in_specs=[
            pl.BlockSpec(memory_space=pl.ANY),
            pl.BlockSpec(memory_space=pl.ANY),
            pl.BlockSpec(memory_space=pltpu.VMEM),
        ],
        out_specs=[
            pl.BlockSpec(memory_space=pltpu.VMEM),
            pl.BlockSpec(memory_space=pl.ANY),
            pl.BlockSpec(memory_space=pl.ANY),
        ],
        scratch_shapes=scratch,
        compiler_params=pltpu.CompilerParams(
            collective_id=0, has_side_effects=True, vmem_limit_bytes=63 * 2**20
        ),
    )(query_embed, gist_embed, pos)
    loss, qg, gg = pl.pallas_call(
        hand_on,
        out_shape=[
            jax.ShapeDtypeStruct((1, 1), F32),
            jax.ShapeDtypeStruct((2048, 128), F32),
            jax.ShapeDtypeStruct((1024, 256), F32),
        ],
        in_specs=[
            pl.BlockSpec(memory_space=pltpu.VMEM),
            pl.BlockSpec(memory_space=pl.ANY),
            pl.BlockSpec(memory_space=pl.ANY),
        ],
        out_specs=[
            pl.BlockSpec(memory_space=pltpu.SMEM),
            pl.BlockSpec(memory_space=pl.ANY),
            pl.BlockSpec(memory_space=pl.ANY),
        ],
        scratch_shapes=[vm((2048, 128), F32), vm((1024, 256), F32), dma((2, 4, 2))],
    )(loss, qg.reshape(2048, 128), gg)
    return loss[0, 0], qg, gg


def solution(mesh):
    in_specs = (P("row", "col"), P("col", "row"), P("row"))
    out_specs = (P(), P("row", "col"), P("col", "row"))
    return jax.shard_map(
        on_device, mesh=mesh, in_specs=in_specs, out_specs=out_specs, check_vma=False
    )
```

time: 117 us -> 106 us (0.906)
  Pallas kernels: 116 us -> 104 us
    pallas_call x1, Pallas kernels: 112 us -> 101 us  [on_device(): pl.pallas_call(kernel, out_shape=[jax.ShapeDtypeStruct((8, 128), F32), ja...]
where the time goes in v3:
time: 106 us; the launch traced here: 105 us
  Pallas kernels  104 us (98%)
    pallas_call x1, Pallas kernels, on_device(): pl.pallas_call(kernel, out_shape=[jax.ShapeDtypeStruct((8, 128), F32), ja...  101 us
    pallas_call x1, Pallas kernels, on_device(): pl.pallas_call(hand_on, out_shape=[jax.ShapeDtypeStruct((1, 1), F32), jax...  3.59 us

profile of v3, /device:TPU:1, one launch (start us, length us, event | category | flops | bytes accessed | tf_op | source)
XLA Modules:
  0.0 105.3 jit_solution(6244625536996955624)
XLA Ops:
  0.6 100.9 %shard_map.58 = (f32[8,128]{1,0:T(8,128)}, f32[4,512,128]{2,1,0:T(8,128)}, f32[1024,256]{1,0:T(8,128)}) custom-call(bf16[2048,128]{1,0:T(8,128)(2,1)} %q_ref.1, bf16[1024,256]{1,0:T(8,128)(2,1)} %g_ref.1, s32[16,128]{1,0:T(8,128)} %bitcast.4), custom_call_target="tpu_custom_call" | custom-call | tf_op jit(solution)/shard_map/pallas_call | solution.py:754
  101.5 3.6 %shard_map.59 = (f32[1,1]{1,0:T(1,128)}, f32[2048,128]{1,0:T(8,128)}, f32[1024,256]{1,0:T(8,128)}) custom-call(f32[8,128]{1,0:T(8,128)} %get-tuple-element.9.loss_in, f32[2048,128]{1,0:T(8,128)} %bitcast.3, f32[1024,256]{1,0:T(8,128)} %get-tuple-element.11.gg_in), custom_call_target="tpu_custom_call" | custom-call | tf_op jit(solution)/shard_map/pallas_call | solution.py:776

commit v4 on v3

--- a/solution.py
+++ b/solution.py
@@ -328,6 +328,14 @@
     logits(3, (0, 1, 2, 3), False)
     stats(2)
     stats(3)
+    for c in range(16):
+        peak = jnp.max(mc[c], axis=0, keepdims=True)
+        one = jnp.sum(sc[c] * jnp.exp2(mc[c] - peak), axis=0, keepdims=True)
+        colst0[0, c // 8, 0, pl.ds(c % 8, 1), :] = peak
+        colst0[0, c // 8, 1, pl.ds(c % 8, 1), :] = one
+    ccopy = rc(colst0.at[0], colst0.at[1], ms.at[3], mv.at[4], core)
+    ccopy.start()
+
     for a in range(8):
         rb = pl.ds((a % 4) * 128, 128)
         tt = qout[0, a // 4, rb, :].T
@@ -335,14 +343,6 @@
         total = qout[1, a // 4, rb, :].T
         ml[pl.ds(a, 1), :] = peak
         sl[pl.ds(a, 1), :] = jnp.sum(total * jnp.exp2(tt - peak), axis=0, keepdims=True)
-
-    for c in range(16):
-        peak = jnp.max(mc[c], axis=0, keepdims=True)
-        one = jnp.sum(sc[c] * jnp.exp2(mc[c] - peak), axis=0, keepdims=True)
-        colst0[0, c // 8, 0, pl.ds(c % 8, 1), :] = peak
-        colst0[0, c // 8, 1, pl.ds(c % 8, 1), :] = one
-    ccopy = rc(colst0.at[0], colst0.at[1], ms.at[3], mv.at[4], core)
-    ccopy.start()
 
     me_row = e * 4 + z
     rowst[me_row, 0] = ml[...]
@@ -365,6 +365,10 @@
         rc(colst.at[y], colst.at[4 + y], cs_, cv_, to).start()
     kall = rc(colst.at[pl.ds(0, 7)], colst.at[pl.ds(0, 7)], cs_, cv_, part_g)
 
+    for a in range(8):
+        r = pl.ds((a % 4) * 128, 128)
+        pos = posbuf[h, pl.ds(k * 8 + a, 1), :].astype(F32)
+        qout[1, a // 4, r, :] = jnp.broadcast_to(pos, (128, 128)).T
     rall.wait()
     peak = rowst[0, 0]
     for n in range(1, 8):
@@ -375,6 +379,9 @@
     row_lse = peak + jnp.log2(tot)
     ml[...] = row_lse
 
+    for a in range(8):
+        r = pl.ds((a % 4) * 128, 128)
+        qout[0, a // 4, r, :] = jnp.broadcast_to(ml[pl.ds(a, 1), :], (128, 128)).T
     kall.wait()
     for i in range(2):
         peak = colst[0, i, 0]
@@ -387,11 +394,6 @@
             tot = tot + (a0 + a1)
         cl_t[pl.ds(i * 8, 8), :] = peak + jnp.log2(tot)
 
-    for a in range(8):
-        r = pl.ds((a % 4) * 128, 128)
-        qout[0, a // 4, r, :] = jnp.broadcast_to(ml[pl.ds(a, 1), :], (128, 128)).T
-        pos = posbuf[h, pl.ds(k * 8 + a, 1), :].astype(F32)
-        qout[1, a // 4, r, :] = jnp.broadcast_to(pos, (128, 128)).T
     lane = lax.broadcasted_iota(jnp.int32, (1, 128), 1)
     first = [(x * 4 + z) * 1024, (xo * 4 + z) * 1024]
 
@@ -418,20 +420,23 @@
     lse_part = jnp.where(sub == me_row, row_lse, 0.0) + jnp.where(sub == y * 2 + k, cl_t[0:8, :], 0.0)
     loss_now = {}
 
-    def loss_begin(n, v, peers, slot, mine):
+    def loss_begin(n, v, slot, mine, count, to):
         lossbuf[slot + mine] = v
-        dst = slot + (mine if len(peers) > 1 else 1)
-        for to in peers:
-            rc(lossbuf.at[slot + mine], lossbuf.at[dst], ls.at[n], lv.at[n], to).start()
-        got = lossbuf.at[pl.ds(slot, len(peers))]
-        loss_now[n] = rc(got, got, ls.at[n], lv.at[n], peers[0])
+        for dst, other in to:
+            rc(lossbuf.at[slot + mine], lossbuf.at[slot + dst], ls.at[n], lv.at[n], other).start()
+        got = lossbuf.at[pl.ds(slot, count - 1)]
+        loss_now[n] = rc(got, got, ls.at[n], lv.at[n], core)
 
     def loss_end(n, slot, count):
         loss_now[n].wait()
         v = [lossbuf[slot + i] for i in range(count)]
-        return v[0] + v[1] if count == 2 else (v[0] + v[1]) + (v[2] + v[3])
-
-    zall, yall = [list(p.values()) for p in (zpeer, ypeer)]
+        while len(v) > 1:
+            v = [v[i] + v[i + len(v) // 2] for i in range(len(v) // 2)]
+        return v[0]
+
+    to_a = [(me_row, to) for to in list(zpeer.values()) + list(zipeer.values()) + [part_q]]
+    to_b = [(y, to) for to in ypeer.values()]
+    to_b += [(4 + y, to) for to in list(yopeer.values()) + [part_g]]
 
     def grad_q(t):
         g = jnp.concatenate(
@@ -590,44 +595,38 @@
     grad_g_sum(3)
     gside.outer(3)
     hits = (pacc[0] + pacc[1]) + (pacc[2] + pacc[3])
-    loss_begin(0, (lse_part - hits) * LN2, [core], 0, 0)
+    loss_begin(0, (lse_part - hits) * LN2, 0, 0, 2, [(1, core)])
     grad_g_other(2)
     grad_q(2)
     qside.outer(2)
     grad_g_own(2)
     grad_g_sum(2)
     gside.outer(2)
-    loss = loss_end(0, 0, 2)
-    loss_begin(1, loss, [part_q], 2, 0)
+    loss_begin(1, loss_end(0, 0, 2), 2, me_row, 8, to_a)
     grad_g_other(1)
     grad_q(1)
     qside.inner(1)
     qside.across(3)
-    loss = loss_end(1, 2, 2)
-    loss_begin(2, loss, [part_g], 4, 0)
     grad_g_own(1)
     grad_g_sum(1)
     gside.inner(1)
     gside.across(3)
-    loss = loss_end(2, 4, 2)
-    loss_begin(3, loss, zall, 6, z)
     grad_g_other(0)
     grad_q(0)
     qside.inner(0)
     qside.late(1)
-    loss = loss_end(3, 6, 4)
-    loss_begin(4, loss, yall, 10, y)
+    loss_begin(2, loss_end(1, 2, 8), 10, y, 8, to_b)
     grad_g_own(0)
     grad_g_sum(0)
     gside.inner(0)
     gside.late(1)
     qside.across(2)
     gside.across(2)
-    loss = loss_end(4, 10, 4)
+    qside.late(0)
+    gside.late(0)
+    loss = loss_end(2, 10, 8)
     loss = jnp.sum(jnp.sum(loss, axis=0, keepdims=True), axis=1, keepdims=True)
     loss_ref[...] = jnp.broadcast_to(loss * (1.0 / 32768.0), (8, 128))
-    qside.late(0)
-    gside.late(0)
     for t in (1, 0):
         xmsg[t].wait_send()
 
@@ -738,14 +737,14 @@
         vm((4, 4, 512, 256), F32),
         vm((2, 2, 512, 128), F32),
         vm((2, 2, 528, 128), I16),
-        vm((14, 8, 128), F32),
+        vm((18, 8, 128), F32),
         dma((4,)), dma((NSLOT,)),
         dma((4,)), dma((NSLOT,)),
         dma((3,)), dma((3,)),
         dma((5,)), dma((7,)),
         dma, dma,
         dma, dma,
-        dma((5,)), dma((5,)),
+        dma((3,)), dma((3,)),
         dma((2,)), dma((4,)),
         dma((4,)),
         dma((4,)),

time: 106 us -> 104 us (0.981)
    pallas_call x1, Pallas kernels: 101 us -> 99.6 us  [on_device(): pl.pallas_call(kernel, out_shape=[jax.ShapeDtypeStruct((8, 128), F32), ja...]
where the time goes in v4:
time: 104 us
  Pallas kernels  103 us (99%)
    pallas_call x1, Pallas kernels, on_device(): pl.pallas_call(kernel, out_shape=[jax.ShapeDtypeStruct((8, 128), F32), ja...  99.6 us
    pallas_call x1, Pallas kernels, on_device(): pl.pallas_call(hand_on, out_shape=[jax.ShapeDtypeStruct((1, 1), F32), jax...  3.59 us

profile of v4, /device:TPU:1, one launch (start us, length us, event | category | flops | bytes accessed | tf_op | source)
XLA Modules:
  0.0 104.0 jit_solution(16168580542499653068)
XLA Ops:
  0.6 99.6 %shard_map.58 = (f32[8,128]{1,0:T(8,128)}, f32[4,512,128]{2,1,0:T(8,128)}, f32[1024,256]{1,0:T(8,128)}) custom-call(bf16[2048,128]{1,0:T(8,128)(2,1)} %q_ref.1, bf16[1024,256]{1,0:T(8,128)(2,1)} %g_ref.1, s32[16,128]{1,0:T(8,128)} %bitcast.4), custom_call_target="tpu_custom_call" | custom-call | tf_op jit(solution)/shard_map/pallas_call | solution.py:753
  100.2 3.6 %shard_map.59 = (f32[1,1]{1,0:T(1,128)}, f32[2048,128]{1,0:T(8,128)}, f32[1024,256]{1,0:T(8,128)}) custom-call(f32[8,128]{1,0:T(8,128)} %get-tuple-element.9.loss_in, f32[2048,128]{1,0:T(8,128)} %bitcast.3, f32[1024,256]{1,0:T(8,128)} %get-tuple-element.11.gg_in), custom_call_target="tpu_custom_call" | custom-call | tf_op jit(solution)/shard_map/pallas_call | solution.py:775

commit v5 on v4

--- a/solution.py
+++ b/solution.py
@@ -617,16 +617,13 @@
     qside.late(1)
     loss_begin(2, loss_end(1, 2, 8), 10, y, 8, to_b)
     grad_g_own(0)
+    qside.across(2)
     grad_g_sum(0)
     gside.inner(0)
     gside.late(1)
-    qside.across(2)
     gside.across(2)
     qside.late(0)
     gside.late(0)
-    loss = loss_end(2, 10, 8)
-    loss = jnp.sum(jnp.sum(loss, axis=0, keepdims=True), axis=1, keepdims=True)
-    loss_ref[...] = jnp.broadcast_to(loss * (1.0 / 32768.0), (8, 128))
     for t in (1, 0):
         xmsg[t].wait_send()
 
@@ -660,6 +657,9 @@
         out_core.start()
 
     puts += [put_g(0, u) for u in (1, 0)]
+    loss = loss_end(2, 10, 8)
+    loss = jnp.sum(jnp.sum(loss, axis=0, keepdims=True), axis=1, keepdims=True)
+    loss_ref[...] = jnp.broadcast_to(loss * (1.0 / 32768.0), (8, 128))
 
     @pl.when(h == k)
     def _():

time: 104 us -> 104 us (level)
  no operation moved by 1% of the time
where the time goes in v5:
time: 104 us
  Pallas kernels  103 us (99%)
    pallas_call x1, Pallas kernels, on_device(): pl.pallas_call(kernel, out_shape=[jax.ShapeDtypeStruct((8, 128), F32), ja...  99.6 us
    pallas_call x1, Pallas kernels, on_device(): pl.pallas_call(hand_on, out_shape=[jax.ShapeDtypeStruct((1, 1), F32), jax...  3.59 us

profile of v5, /device:TPU:1, one launch (start us, length us, event | category | flops | bytes accessed | tf_op | source)
XLA Modules:
  0.0 104.0 jit_solution(11060366942579577988)
XLA Ops:
  0.6 99.6 %shard_map.58 = (f32[8,128]{1,0:T(8,128)}, f32[4,512,128]{2,1,0:T(8,128)}, f32[1024,256]{1,0:T(8,128)}) custom-call(bf16[2048,128]{1,0:T(8,128)(2,1)} %q_ref.1, bf16[1024,256]{1,0:T(8,128)(2,1)} %g_ref.1, s32[16,128]{1,0:T(8,128)} %bitcast.4), custom_call_target="tpu_custom_call" | custom-call | tf_op jit(solution)/shard_map/pallas_call | solution.py:753
  100.2 3.6 %shard_map.59 = (f32[1,1]{1,0:T(1,128)}, f32[2048,128]{1,0:T(8,128)}, f32[1024,256]{1,0:T(8,128)}) custom-call(f32[8,128]{1,0:T(8,128)} %get-tuple-element.9.loss_in, f32[2048,128]{1,0:T(8,128)} %bitcast.3, f32[1024,256]{1,0:T(8,128)} %get-tuple-element.11.gg_in), custom_call_target="tpu_custom_call" | custom-call | tf_op jit(solution)/shard_map/pallas_call | solution.py:775
